TPU v7x, 32 devices: a whole 2x2x4 slice. The times are simulated.
32 devices in a mesh: dp: 8 (over y, x, core), tensor: 4 (over z).
Axes of the slice: x: 2, y: 2, z: 4, core: 2. Of those that a mesh axis runs over, the one named last changes fastest.
Arguments:
- hidden_in: bfloat16 [16384, 768], P(('dp', 'tensor')), may hold values from -6 to 6
- lengths: int32 [16], P('dp'), may hold values from 64 to 1024, as said below
- ln1_gain: bfloat16 [768], replicated, may hold values from 0.099609375 to 1.8984375
- ln1_bias: bfloat16 [768], replicated, may hold values from -3 to 3
- w_qkv: bfloat16 [768, 3, 768], P(None, None, 'tensor'), may hold values from -0.21875 to 0.21875
- b_query: bfloat16 [768], P('tensor'), may hold values from -3 to 3
- b_value: bfloat16 [768], P('tensor'), may hold values from -3 to 3
- w_out: bfloat16 [768, 768], P('tensor'), may hold values from -2.5 to 2.5
- b_out: bfloat16 [768], replicated, may hold values from -3 to 3
- ln2_gain: bfloat16 [768], replicated, may hold values from 0.099609375 to 1.8984375
- ln2_bias: bfloat16 [768], replicated, may hold values from -3 to 3
- w_fc: bfloat16 [768, 3072], P(None, 'tensor'), may hold values from -0.21875 to 0.21875
- b_fc: bfloat16 [3072], P('tensor'), may hold values from -3 to 3
- w_proj: bfloat16 [3072, 768], P('tensor'), may hold values from -0.4375 to 0.4375
- b_proj: bfloat16 [768], replicated, may hold values from -3 to 3
- out_grad: bfloat16 [16384, 768], P(('dp', 'tensor')), may hold values from -6 to 6
Outputs:
- block_out: bfloat16 [16384, 768], P(('dp', 'tensor'))
- grad_input: bfloat16 [16384, 768], P(('dp', 'tensor'))
- grad_ln1_gain: float32 [768], replicated
- grad_ln1_bias: float32 [768], replicated
- grad_w_qkv: float32 [768, 3, 768], P(None, None, 'tensor')
- grad_b_query: float32 [768], P('tensor')
- grad_b_value: float32 [768], P('tensor')
- grad_w_out: float32 [768, 768], P('tensor')
- grad_b_out: float32 [768], replicated
- grad_ln2_gain: float32 [768], replicated
- grad_ln2_bias: float32 [768], replicated
- grad_w_fc: float32 [768, 3072], P(None, 'tensor')
- grad_b_fc: float32 [3072], P('tensor')
- grad_w_proj: float32 [3072, 768], P('tensor')
- grad_b_proj: float32 [768], replicated
Inputs may be any that keep to these rules, and one draw needn't show every extreme that they name: `lengths`: valid tokens of each sequence; one of the 16 sequences has exactly 1024.
All inputs are finite; a program needn't handle non-finite values.
Results may differ from a plain program's by a relative error of at most 0.018.
Values may be sent and summed in bfloat16 or wider, within the bound.
A program may use at most 128 MiB of HBM per device.

v0:
```python
import jax
import jax.numpy as jnp
from jax import lax
from jax.sharding import PartitionSpec as P

HEAD_DIM = 64


eps_norm = 1e-05
masked_score = -1e30


def layer_norm(value, gain, shift):
    row_mean = jnp.mean(value, axis=-1, keepdims=True)
    centred = value - row_mean
    variance = jnp.mean(centred * centred, axis=-1, keepdims=True)
    return centred * lax.rsqrt(variance + eps_norm) * gain + shift


def gelu_tanh(value):
    return jax.nn.gelu(value, approximate=True)


def key_count(block_total):
    return jnp.int32(block_total)


def block_scores(query_block, key_rows, length, row_ids, key_index, block_size):
    key_start = key_index * block_size
    key_block = lax.dynamic_slice_in_dim(key_rows, key_start, block_size, 0)
    score_scale = query_block.shape[2] ** (-0.5)
    raw_scores = (
        jnp.einsum("qhe,khe->hqk", query_block, key_block, preferred_element_type=jnp.float32)
        * score_scale
    )
    col_ids = key_start + lax.iota(jnp.int32, block_size)
    allowed = (col_ids[None, :] <= row_ids[:, None]) & (col_ids[None, :] < length)
    return (jnp.where(allowed[None], raw_scores, masked_score), key_start)


def attend_sequence(queries, key_rows, value_rows, length, block_size):
    seq_span, head_count, head_size = queries.shape
    block_total = seq_span // block_size

    def one_block(query_index):
        query_start = query_index * block_size
        query_block = lax.dynamic_slice_in_dim(queries, query_start, block_size, 0)
        row_ids = query_start + lax.iota(jnp.int32, block_size)
        visits = key_count(block_total)

        def first_pass(key_index, carried):
            row_top, row_total = carried
            scores, key_start = block_scores(
                query_block, key_rows, length, row_ids, key_index, block_size
            )
            new_top = jnp.maximum(row_top, jnp.max(scores, axis=-1))
            row_total = row_total * jnp.exp(row_top - new_top) + jnp.sum(
                jnp.exp(scores - new_top[..., None]), axis=-1
            )
            return (new_top, row_total)

        start_top = jnp.full((head_count, block_size), masked_score, jnp.float32)
        start_total = jnp.zeros((head_count, block_size), jnp.float32)
        row_top, row_total = lax.fori_loop(0, visits, first_pass, (start_top, start_total))
        log_total = row_top + jnp.log(row_total)

        def second_pass(key_index, summed):
            scores, key_start = block_scores(
                query_block, key_rows, length, row_ids, key_index, block_size
            )
            probs = jnp.exp(scores - log_total[..., None]).astype(jnp.bfloat16)
            value_block = lax.dynamic_slice_in_dim(value_rows, key_start, block_size, 0)
            return summed + jnp.einsum(
                "hqk,khe->qhe", probs, value_block, preferred_element_type=jnp.float32
            )

        context = lax.fori_loop(
            0, visits, second_pass, jnp.zeros((block_size, head_count, head_size), jnp.float32)
        )
        return (context, log_total)

    context, log_total = lax.map(one_block, jnp.arange(block_total, dtype=jnp.int32))
    return (context.reshape(seq_span, head_count, head_size), log_total)


def attend_backward(
    queries, key_rows, value_rows, length, log_total, row_delta, grad_context, block_size
):
    seq_span, head_count, head_size = queries.shape
    block_total = seq_span // block_size
    score_scale = head_size ** (-0.5)

    def one_block(query_index, carried):
        grad_queries, grad_keys, grad_values = carried
        query_start = query_index * block_size
        query_block = lax.dynamic_slice_in_dim(queries, query_start, block_size, 0)
        grad_block = lax.dynamic_slice_in_dim(grad_context, query_start, block_size, 0)
        row_ids = query_start + lax.iota(jnp.int32, block_size)
        total_block = lax.dynamic_index_in_dim(log_total, query_index, 0, keepdims=False)
        delta_block = lax.dynamic_slice_in_dim(row_delta, query_start, block_size, 1)
        visits = key_count(block_total)

        def inner_pass(key_index, inner_carried):
            query_sum, grad_keys, grad_values = inner_carried
            scores, key_start = block_scores(
                query_block, key_rows, length, row_ids, key_index, block_size
            )
            probs = jnp.exp(scores - total_block[..., None])
            key_block = lax.dynamic_slice_in_dim(key_rows, key_start, block_size, 0)
            value_block = lax.dynamic_slice_in_dim(value_rows, key_start, block_size, 0)
            grad_probs = jnp.einsum(
                "qhe,khe->hqk", grad_block, value_block, preferred_element_type=jnp.float32
            )
            grad_scores = (probs * (grad_probs - delta_block[..., None]) * score_scale).astype(
                jnp.bfloat16
            )
            query_sum = query_sum + jnp.einsum(
                "hqk,khe->qhe", grad_scores, key_block, preferred_element_type=jnp.float32
            )
            key_piece = jnp.einsum(
                "hqk,qhe->khe", grad_scores, query_block, preferred_element_type=jnp.float32
            )
            value_piece = jnp.einsum(
                "hqk,qhe->khe",
                probs.astype(jnp.bfloat16),
                grad_block,
                preferred_element_type=jnp.float32,
            )
            grad_keys = lax.dynamic_update_slice_in_dim(
                grad_keys,
                lax.dynamic_slice_in_dim(grad_keys, key_start, block_size, 0) + key_piece,
                key_start,
                0,
            )
            grad_values = lax.dynamic_update_slice_in_dim(
                grad_values,
                lax.dynamic_slice_in_dim(grad_values, key_start, block_size, 0) + value_piece,
                key_start,
                0,
            )
            return (query_sum, grad_keys, grad_values)

        start_sum = jnp.zeros((block_size, head_count, head_size), jnp.float32)
        query_sum, grad_keys, grad_values = lax.fori_loop(
            0, visits, inner_pass, (start_sum, grad_keys, grad_values)
        )
        grad_queries = lax.dynamic_update_slice_in_dim(grad_queries, query_sum, query_start, 0)
        return (grad_queries, grad_keys, grad_values)

    zero_rows = jnp.zeros((seq_span, head_count, head_size), jnp.float32)
    return lax.fori_loop(0, block_total, one_block, (zero_rows, zero_rows, zero_rows))


def flatten_grads(arrays, device_count):
    flat_grads = jnp.concatenate([array.reshape(-1) for array in arrays])
    padding = -flat_grads.shape[0] % device_count
    return jnp.concatenate([flat_grads, jnp.zeros((padding,), jnp.float32)])


def unflatten_grads(flat_grads, templates):
    unpacked = []
    offset = 0
    for array in templates:
        amount = array.size
        unpacked.append(flat_grads[offset : offset + amount].reshape(array.shape))
        offset = offset + amount
    return unpacked


def body(
    hidden_in,
    lengths,
    ln1_gain,
    ln1_bias,
    w_qkv,
    b_query,
    b_value,
    w_out,
    b_out,
    ln2_gain,
    ln2_bias,
    w_fc,
    b_fc,
    w_proj,
    b_proj,
    out_grad,
):
    share_rows = hidden_in.shape[0]
    tensor_count = lax.axis_size("tensor")
    data_count = lax.axis_size("dp")
    group_rows = share_rows * tensor_count
    seq_count = lengths.shape[0]
    seq_span = group_rows // seq_count
    block_size = min(512, seq_span // 2)
    local_heads = w_qkv.shape[2] // HEAD_DIM
    shape_four = (seq_count, seq_span, local_heads, HEAD_DIM)
    own_start = lax.axis_index("tensor") * share_rows
    gain_one = ln1_gain.astype(jnp.float32)
    shift_one = ln1_bias.astype(jnp.float32)
    gain_two = ln2_gain.astype(jnp.float32)
    shift_two = ln2_bias.astype(jnp.float32)
    inputs = hidden_in.astype(jnp.float32)
    normed_share, norm_one_back = jax.vjp(layer_norm, inputs, gain_one, shift_one)
    normed_one = lax.all_gather(normed_share.astype(jnp.bfloat16), "tensor", axis=0, tiled=True)
    mixed_qkv = jnp.einsum("td,dcn->tcn", normed_one, w_qkv, preferred_element_type=jnp.float32)
    queries = (
        (mixed_qkv[:, 0] + b_query.astype(jnp.float32)).astype(jnp.bfloat16).reshape(shape_four)
    )
    key_rows = mixed_qkv[:, 1].astype(jnp.bfloat16).reshape(shape_four)
    value_rows = (
        (mixed_qkv[:, 2] + b_value.astype(jnp.float32)).astype(jnp.bfloat16).reshape(shape_four)
    )

    def forward_one(inputs_one):
        return attend_sequence(
            inputs_one[0], inputs_one[1], inputs_one[2], inputs_one[3], block_size
        )

    context_exact, log_total = lax.map(forward_one, (queries, key_rows, value_rows, lengths))
    context_exact = context_exact.reshape(group_rows, -1)
    context = context_exact.astype(jnp.bfloat16)
    attn_share = lax.psum_scatter(
        jnp.dot(context, w_out, preferred_element_type=jnp.float32),
        "tensor",
        scatter_dimension=0,
        tiled=True,
    )
    middle = inputs + attn_share + b_out.astype(jnp.float32)
    normed_share_two, norm_two_back = jax.vjp(layer_norm, middle, gain_two, shift_two)
    normed_two = lax.all_gather(normed_share_two.astype(jnp.bfloat16), "tensor", axis=0, tiled=True)
    pre_act = jnp.dot(normed_two, w_fc, preferred_element_type=jnp.float32) + b_fc.astype(
        jnp.float32
    )
    activation, gelu_back = jax.vjp(gelu_tanh, pre_act)
    activation = activation.astype(jnp.bfloat16)
    mlp_share = lax.psum_scatter(
        jnp.dot(activation, w_proj, preferred_element_type=jnp.float32),
        "tensor",
        scatter_dimension=0,
        tiled=True,
    )
    result_share = middle + mlp_share + b_proj.astype(jnp.float32)
    row_index = own_start + lax.iota(jnp.int32, share_rows)
    seq_of_row = row_index // seq_span
    position = row_index % seq_span
    own_length = jnp.sum(
        jnp.where(
            seq_of_row[:, None] == jnp.arange(seq_count, dtype=jnp.int32)[None, :],
            lengths[None, :],
            0,
        ),
        axis=1,
    )
    valid_rows = (position < own_length).astype(jnp.float32)[:, None]
    block_out = (result_share * valid_rows).astype(jnp.bfloat16)
    grad_top = out_grad.astype(jnp.float32) * valid_rows
    grad_mlp = lax.all_gather(grad_top.astype(jnp.bfloat16), "tensor", axis=0, tiled=True)
    grad_w_proj = jnp.einsum("tf,td->fd", activation, grad_mlp, preferred_element_type=jnp.float32)
    grad_act = jnp.einsum("td,fd->tf", grad_mlp, w_proj, preferred_element_type=jnp.float32)
    grad_pre = gelu_back(grad_act)[0].astype(jnp.bfloat16)
    grad_b_fc = jnp.sum(grad_pre.astype(jnp.float32), axis=0)
    grad_w_fc = jnp.einsum("td,tf->df", normed_two, grad_pre, preferred_element_type=jnp.float32)
    grad_normed_two = lax.psum_scatter(
        jnp.einsum("tf,df->td", grad_pre, w_fc, preferred_element_type=jnp.float32),
        "tensor",
        scatter_dimension=0,
        tiled=True,
    )
    grad_mid_norm, grad_gain_two, grad_shift_two = norm_two_back(grad_normed_two)
    grad_middle = grad_top + grad_mid_norm
    mlp_parts = (grad_w_fc, grad_b_fc, grad_w_proj)
    grad_attn = lax.all_gather(grad_middle.astype(jnp.bfloat16), "tensor", axis=0, tiled=True)
    grad_w_out = jnp.einsum("tc,td->cd", context, grad_attn, preferred_element_type=jnp.float32)
    grad_context = jnp.einsum(
        "td,cd->tc", grad_attn, w_out, preferred_element_type=jnp.float32
    ).astype(jnp.bfloat16)
    row_delta = jnp.sum(
        (grad_context.astype(jnp.float32) * context_exact).reshape(shape_four), axis=-1
    )
    row_delta = jnp.swapaxes(row_delta, 1, 2)

    def backward_one(inputs_one):
        return attend_backward(
            inputs_one[0],
            inputs_one[1],
            inputs_one[2],
            inputs_one[3],
            inputs_one[4],
            inputs_one[5],
            inputs_one[6],
            block_size,
        )

    grad_queries, grad_keys, grad_values = lax.map(
        backward_one,
        (
            queries,
            key_rows,
            value_rows,
            lengths,
            log_total,
            row_delta,
            grad_context.reshape(shape_four),
        ),
    )
    grad_mixed = jnp.stack(
        [
            grad_queries.reshape(group_rows, -1),
            grad_keys.reshape(group_rows, -1),
            grad_values.reshape(group_rows, -1),
        ],
        axis=1,
    ).astype(jnp.bfloat16)
    grad_b_query = jnp.sum(grad_mixed[:, 0].astype(jnp.float32), axis=0)
    grad_b_value = jnp.sum(grad_mixed[:, 2].astype(jnp.float32), axis=0)
    grad_w_qkv = jnp.einsum(
        "td,tcn->dcn", normed_one, grad_mixed, preferred_element_type=jnp.float32
    )
    grad_normed_one = lax.psum_scatter(
        jnp.einsum("tcn,dcn->td", grad_mixed, w_qkv, preferred_element_type=jnp.float32),
        "tensor",
        scatter_dimension=0,
        tiled=True,
    )
    grad_in_norm, grad_gain_one, grad_shift_one = norm_one_back(grad_normed_one)
    grad_input = (grad_middle + grad_in_norm).astype(jnp.bfloat16)
    common_grads = lax.psum(
        (
            grad_gain_one,
            grad_shift_one,
            grad_gain_two,
            grad_shift_two,
            jnp.sum(grad_middle, axis=0),
            jnp.sum(grad_top, axis=0),
        ),
        ("dp", "tensor"),
    )
    attn_parts = (grad_w_qkv, grad_b_query, grad_b_value, grad_w_out)
    every_flat = flatten_grads(attn_parts + mlp_parts, data_count)
    every_summed = lax.psum_scatter(every_flat, "dp", scatter_dimension=0, tiled=True)
    every_whole = lax.all_gather(every_summed, "dp", axis=0, tiled=True)
    every_list = unflatten_grads(every_whole, attn_parts + mlp_parts)
    attn_list = every_list[0:4]
    mlp_list = every_list[4:7]
    return (
        block_out,
        grad_input,
        common_grads[0],
        common_grads[1],
        attn_list[0],
        attn_list[1],
        attn_list[2],
        attn_list[3],
        common_grads[4],
        common_grads[2],
        common_grads[3],
        mlp_list[0],
        mlp_list[1],
        mlp_list[2],
        common_grads[5],
    )


def solution(mesh):
    in_specs = (
        P(("dp", "tensor"), None),
        P("dp"),
        P(),
        P(),
        P(None, None, "tensor"),
        P("tensor"),
        P("tensor"),
        P("tensor", None),
        P(),
        P(),
        P(),
        P(None, "tensor"),
        P("tensor"),
        P("tensor", None),
        P(),
        P(("dp", "tensor"), None),
    )
    out_specs = (
        P(("dp", "tensor"), None),
        P(("dp", "tensor"), None),
        P(),
        P(),
        P(None, None, "tensor"),
        P("tensor"),
        P("tensor"),
        P("tensor", None),
        P(),
        P(),
        P(),
        P(None, "tensor"),
        P("tensor"),
        P("tensor", None),
        P(),
    )
    return jax.shard_map(body, mesh=mesh, in_specs=in_specs, out_specs=out_specs, check_vma=False)
```

profile of v0, /device:TPU:1, one launch (start us, length us, event | category | flops | bytes accessed | tf_op | source)
XLA Modules:
  0.0 1307.9 jit_solution(2404076603059768270)
XLA Ops:
  13.8 65.5 %all-gather.5.cloned.1.call-done = bf16[2048,768]{1,0:T(8,128)(2,1)} async-done(((bf16[512,768]{1,0:T(8,128)(2,1)}), bf16[2048,768]{1,0:T(8,128)(2,1)}) %all-gather.5.cloned.1.call-update) | async-done | bytes 3145744 | tf_op jit(solution)/shard_map/all_gather | solution.py:204
  98.9 90.9 %while.114 = (s32[]{:T(128)}, f32[2,1024,3,64]{1,0,3,2:T(2,128)}, f32[2,2,3,512]{3,2,1,0:T(4,128)}, bf16[2,1024,3,64]{1,3,2,0:T(8,128)(2,1)}, bf16[2,1024,3,64]{...) while((s32[]{:T(128)}, f32[2,1024,3,64]{1,0,3,2:T(2,128)}, ...), condition=%wide.region_11.12_spmd, body=%wide.region_2.11_spmd.sunk | while | flops 311899136 | bytes 17799904 | solution.py:219
  102.4 23.2 %while.117 = (s32[]{:T(128)}, f32[2,512,3,64]{1,3,2,0:T(8,128)}, f32[2,3,512]{2,1,0:T(4,128)S(1)}, s32[2]{0:T(128)S(1)}, bf16[1024,3,64]{0,2,1:T(8,128)(2,1)S(1)...) while((s32[]{:T(128)}, f32[2,512,3,64]{1,3,2,0:T(8,128)}, ...), condition=%wide.region_10.10_spmd, body=%wide.region_3.9_spmd.sunk | while | flops 311899136 | bytes 10692945 | solution.py:82
  103.7 5.0 while.120
  115.3 5.0 while.120
  130.0 14.4 %dynamic_update_slice.59 = f32[2,1024,3,64]{1,0,3,2:T(2,128)} dynamic-update-slice(f32[2,1024,3,64]{1,0,3,2:T(2,128)} %get-tuple-element.1701, f32[1,1024,3,64]{1,0,3,2:T(1,128)} %copy.145, s32[]{:T(128)S(6)} %copy.208, s32[]{:T(128)} %constant.192.clone.1..sunk, s32[]{:T(128)} %constant.192.clone.1..sunk, s32[]{:T(128)} %constant.192.clone.1..sunk) | dynamic-update-slice | bytes 1572868 | tf_op jit(solution)/shard_map/while/body/jit(dynamic_update_index_in_dim)/dynamic_update_slice | solution.py:219
  147.9 23.2 %while.117 = (s32[]{:T(128)}, f32[2,512,3,64]{1,3,2,0:T(8,128)}, f32[2,3,512]{2,1,0:T(4,128)S(1)}, s32[2]{0:T(128)S(1)}, bf16[1024,3,64]{0,2,1:T(8,128)(2,1)S(1)...) while((s32[]{:T(128)}, f32[2,512,3,64]{1,3,2,0:T(8,128)}, ...), condition=%wide.region_10.10_spmd, body=%wide.region_3.9_spmd.sunk | while | flops 311899136 | bytes 10692945 | solution.py:82
  175.5 14.4 %dynamic_update_slice.59 = f32[2,1024,3,64]{1,0,3,2:T(2,128)} dynamic-update-slice(f32[2,1024,3,64]{1,0,3,2:T(2,128)} %get-tuple-element.1701, f32[1,1024,3,64]{1,0,3,2:T(1,128)} %copy.145, s32[]{:T(128)S(6)} %copy.208, s32[]{:T(128)} %constant.192.clone.1..sunk, s32[]{:T(128)} %constant.192.clone.1..sunk, s32[]{:T(128)} %constant.192.clone.1..sunk) | dynamic-update-slice | bytes 1572868 | tf_op jit(solution)/shard_map/while/body/jit(dynamic_update_index_in_dim)/dynamic_update_slice | solution.py:219
  196.9 108.4 %reduce-scatter.5.cloned.1.call-done = f32[512,768]{1,0:T(8,128)} async-done(((f32[2048,768]{1,0:T(8,128)}), f32[512,768]{1,0:T(8,128)}) %reduce-scatter.5.cloned.1.call-update) | async-done | bytes 1572880 | tf_op jit(solution)/shard_map/reduce_scatter | solution.py:222
  312.8 60.6 %all-gather.7.cloned.1.call-done = bf16[2048,768]{1,0:T(8,128)(2,1)} async-done(((bf16[512,768]{1,0:T(8,128)(2,1)}), bf16[2048,768]{1,0:T(8,128)(2,1)}) %all-gather.7.cloned.1.call-update) | async-done | bytes 3145744 | tf_op jit(solution)/shard_map/all_gather | solution.py:230
  373.5 7.5 fusion.101
  380.9 56.7 %all-gather.9.cloned.1.call-done = bf16[2048,768]{1,0:T(8,128)(2,1)} async-done(((bf16[512,768]{1,0:T(8,128)(2,1)}), bf16[2048,768]{1,0:T(8,128)(2,1)}) %all-gather.9.cloned.1.call-update) | async-done | bytes 3145744 | tf_op jit(solution)/shard_map/all_gather | solution.py:257
  437.7 12.5 convert_reduce_fusion
  456.4 7.6 fusion.102
  464.7 101.3 %reduce-scatter.9.cloned.1.call-done = f32[512,768]{1,0:T(8,128)} async-done(((f32[2048,768]{1,0:T(8,128)}), f32[512,768]{1,0:T(8,128)}) %reduce-scatter.9.cloned.1.call-update) | async-done | bytes 1572880 | tf_op jit(solution)/shard_map/reduce_scatter | solution.py:263
  569.1 110.4 %reduce-scatter.7.cloned.1.call-done = f32[512,768]{1,0:T(8,128)} async-done(((f32[2048,768]{1,0:T(8,128)}), f32[512,768]{1,0:T(8,128)}) %reduce-scatter.7.cloned.1.call-update) | async-done | bytes 1572880 | tf_op jit(solution)/shard_map/reduce_scatter | solution.py:236
  686.3 6.9 fusion.104
  696.5 6.9 fusion.105
  706.7 43.3 %all-gather.11.cloned.1.call-done = bf16[2048,768]{1,0:T(8,128)(2,1)} async-done(((bf16[512,768]{1,0:T(8,128)(2,1)}), bf16[2048,768]{1,0:T(8,128)(2,1)}) %all-gather.11.cloned.1.call-update) | async-done | bytes 3145744 | tf_op jit(solution)/shard_map/all_gather | solution.py:272
  759.6 72.8 %while.116 = (s32[]{:T(128)}, bf16[2,1024,3,64]{1,3,2,0:T(8,128)(2,1)}, bf16[2,1024,3,64]{1,3,2,0:T(8,128)(2,1)}, bf16[2,1024,3,64]{1,3,2,0:T(8,128)(2,1)}, bf16...) while((s32[]{:T(128)}, ...), condition=%wide.region_26.27_spmd, body=%wide.region_21.26_spmd.sunk | while | flops 513083392 | bytes 38865028 | solution.py:294
  769.3 24.0 %while.118 = (s32[]{:T(128)}, bf16[1024,3,64]{0,2,1:T(8,128)(2,1)}, f32[1024,3,64]{0,2,1:T(8,128)S(1)}, f32[1024,3,64]{0,2,1:T(8,128)S(1)}, bf16[1024,3,64]{0,2,...) while((s32[]{:T(128)}, bf16[1024,3,64]{0,2,1:T(8,128)(2,1)}, ...), condition=%wide.region_25.25_spmd, body=%wide.region_22.24_spmd.sunk | while | flops 512886784 | bytes 21882512 | solution.py:151
  770.8 9.9 while.119
  782.8 9.9 while.119
  805.6 24.0 %while.118 = (s32[]{:T(128)}, bf16[1024,3,64]{0,2,1:T(8,128)(2,1)}, f32[1024,3,64]{0,2,1:T(8,128)S(1)}, f32[1024,3,64]{0,2,1:T(8,128)S(1)}, bf16[1024,3,64]{0,2,...) while((s32[]{:T(128)}, bf16[1024,3,64]{0,2,1:T(8,128)(2,1)}, ...), condition=%wide.region_25.25_spmd, body=%wide.region_22.24_spmd.sunk | while | flops 512886784 | bytes 21882512 | solution.py:151
  807.0 9.9 while.119
  819.0 9.8 while.119
  856.8 52.6 %concatenate.3 = f32[1770624]{0:T(1024)} concatenate(f32[442368]{0:T(1024)} %reshape.356, f32[192]{0:T(256)S(1)} %convert_reduce_fusion.3, f32[192]{0:T(256)S(1)} %convert_reduce_fusion.2, f32[147456]{0:T(1024)S(1)} %copy-done.16, f32[589824]{0:T(1024)S(1)} %copy-done.13, f32[768]{0:T(1024)S(1)} %copy-done.41, f32[589824]{0:T(1024)} %reshape.359), dimensions={0} | concatenate | bytes 14164992 | tf_op jit(solution)/shard_map/concatenate | solution.py:157
  912.0 109.8 %all-reduce.8.cloned.1.call-done = f32[1770624]{0:T(1024)} async-done(((f32[1770624]{0:T(1024)}), f32[1770624]{0:T(1024)}) %all-reduce.8.cloned.1.call-update) | async-done | bytes 7082512
  1029.9 5.1 convolution_bitcast_fusion.2
  1035.0 106.6 %all-reduce.6.cloned.1.call-done = f32[1770624]{0:T(1024)} async-done(((f32[1770624]{0:T(1024)}), f32[1770624]{0:T(1024)}) %all-reduce.6.cloned.1.call-update) | async-done | bytes 7082512
  1164.8 89.7 %reduce-scatter.11.cloned.1.call-done = f32[512,768]{1,0:T(8,128)} async-done(((f32[2048,768]{1,0:T(8,128)}), f32[512,768]{1,0:T(8,128)}) %reduce-scatter.11.cloned.1.call-update) | async-done | bytes 1572880 | tf_op jit(solution)/shard_map/reduce_scatter | solution.py:319
  1260.0 40.9 %all-reduce.2 = (f32[768]{0:T(1024)}, f32[768]{0:T(1024)}, f32[768]{0:T(1024)}, f32[768]{0:T(1024)}, f32[768]{0:T(1024)}, /*index=5*/f32[768]{0:T(1024)}) all-reduce(f32[768]{0:T(1024)S(1)} %get-tuple-element.726, f32[768]{0:T(1024)S(1)} %get-tuple-element.729, ...), channel_id=1, replica_groups=mesh['dp'=8,'tensor'=4] {'dp','tensor'}, use_global_device_ids=true, to_apply=%region_31.32 | all-reduce | flops 4608 | bytes 36864 | tf_op jit(solution)/shard_map/psum | solution.py:327
  (492 shorter events, 293.7 us)
Async XLA Ops:
  7.2 430.5 %copy-start = (bf16[768,768]{1,0:T(8,128)(2,1)S(1)}, bf16[768,768]{1,0:T(8,128)(2,1)}, u32[]{:S(2)}) copy-start(bf16[768,768]{1,0:T(8,128)(2,1)} %param.43) | copy-start | bytes 3538948
  7.2 5.1 copy-start.6
  7.2 72.0 %all-gather.5.cloned.1.call-start = ((), (), s32[]{:S(2)}) async-start(), calls=%async_computation.4 | async-start | bytes 3932160 | tf_op jit(solution)/shard_map/all_gather | solution.py:204
  8.7 4.9 copy-start.47
  8.7 5.0 copy-start.48
  8.7 70.5 %copy-start.51 = (bf16[768,3,192]{0,2,1:T(8,128)(2,1)S(1)}, bf16[768,3,192]{0,2,1:T(8,128)(2,1)}, u32[]{:S(2)}) copy-start(bf16[768,3,192]{0,2,1:T(8,128)(2,1)} %param.34) | copy-start | bytes 2654212
  8.7 3.5 copy-start.26
  13.6 291.8 %reduce-scatter.5.cloned.1.call-start = ((), (), s32[]{:S(2)}) async-start(), calls=%async_computation.5 | async-start | bytes 7864320 | tf_op jit(solution)/shard_map/reduce_scatter | solution.py:222
  191.9 558.1 %copy-start.2 = (f32[24,8,2,1024]{3,1,2,0:T(8,128)}, f32[24,8,2,1024]{3,1,2,0:T(8,128)S(1)}, u32[]{:S(2)}) copy-start(f32[24,8,2,1024]{3,1,2,0:T(8,128)S(1)} %copy.132) | copy-start | bytes 4718596
  195.6 109.7 %copy-start.7 = (bf16[512,768]{1,0:T(8,128)(2,1)S(1)}, bf16[512,768]{1,0:T(8,128)(2,1)}, u32[]{:S(2)}) copy-start(bf16[512,768]{1,0:T(8,128)(2,1)} %param.30) | copy-start | bytes 2359300
  195.7 177.8 %all-gather.7.cloned.1.call-start = ((), (), s32[]{:S(2)}) async-start(), calls=%async_computation.6 | async-start | bytes 3932160 | tf_op jit(solution)/shard_map/all_gather | solution.py:230
  309.4 128.3 %all-gather.9.cloned.1.call-start = ((), (), s32[]{:S(2)}) async-start(), calls=%async_computation.8 | async-start | bytes 3932160 | tf_op jit(solution)/shard_map/all_gather | solution.py:257
  310.2 373.3 %copy-start.28 = (f32[512]{0:T(512)}, f32[512]{0:T(512)S(1)}, u32[]{:S(2)}) copy-start(f32[512]{0:T(512)S(1)} %fusion.84) | copy-start | bytes 6148
  311.3 254.7 %reduce-scatter.9.cloned.1.call-start = ((), (), s32[]{:S(2)}) async-start(), calls=%async_computation.9 | async-start | bytes 7864320 | tf_op jit(solution)/shard_map/reduce_scatter | solution.py:263
  437.7 14.1 %copy-start.50 = (bf16[768,768]{1,0:T(8,128)(2,1)S(1)}, bf16[768,768]{1,0:T(8,128)(2,1)}, u32[]{:S(2)}) copy-start(bf16[768,768]{1,0:T(8,128)(2,1)} %param.41) | copy-start | bytes 3538948
  456.4 223.1 %reduce-scatter.7.cloned.1.call-start = ((), (), s32[]{:S(2)}) async-start(), calls=%async_computation.7 | async-start | bytes 7864320 | tf_op jit(solution)/shard_map/reduce_scatter | solution.py:236
  464.1 105.0 %copy-start.37 = (f32[512]{0:T(512)S(1)}, f32[512]{0:T(512)}, u32[]{:S(2)}) copy-start(f32[512]{0:T(512)} %copy-done.36) | copy-start | bytes 6148
  464.1 286.0 %all-gather.11.cloned.1.call-start = ((), (), s32[]{:S(2)}) async-start(), calls=%async_computation.10 | async-start | bytes 3932160 | tf_op jit(solution)/shard_map/all_gather | solution.py:272
  686.0 335.8 %all-reduce.8.cloned.1.call-start = ((), (), s32[]{:S(2)}) async-start(), calls=%async_computation.13 | async-start | bytes 14172160
  703.4 46.6 %copy-start.18 = (bf16[192,768]{1,0:T(8,128)(2,1)S(1)}, bf16[192,768]{1,0:T(8,128)(2,1)}, u32[]{:S(2)}) copy-start(bf16[192,768]{1,0:T(8,128)(2,1)} %param.37) | copy-start | bytes 884740
  836.1 3.6 copy-start.19
  852.0 4.8 copy-start.13
  852.0 4.8 copy-start.16
  852.0 4.8 copy-start.41
  909.5 232.1 %all-reduce.6.cloned.1.call-start = ((), (), s32[]{:S(2)}) async-start(), calls=%async_computation.12 | async-start | bytes 14172160
  1028.0 226.5 %reduce-scatter.11.cloned.1.call-start = ((), (), s32[]{:S(2)}) async-start(), calls=%async_computation.11 | async-start | bytes 7864320 | tf_op jit(solution)/shard_map/reduce_scatter | solution.py:319
  1158.7 95.8 %copy-start.8 = (bf16[512,768]{1,0:T(8,128)(2,1)S(1)}, bf16[512,768]{1,0:T(8,128)(2,1)}, u32[]{:S(2)}) copy-start(bf16[512,768]{1,0:T(8,128)(2,1)} %param.30) | copy-start | bytes 2359300
  1158.7 95.8 %copy-start.25 = (f32[768]{0:T(1024)S(1)}, f32[768]{0:T(1024)}, u32[]{:S(2)}) copy-start(f32[768]{0:T(1024)} %copy-done.24) | copy-start | bytes 9220
  1158.7 95.8 %copy-start.27 = (f32[512]{0:T(512)S(1)}, f32[512]{0:T(512)}, u32[]{:S(2)}) copy-start(f32[512]{0:T(512)} %copy-done.26) | copy-start | bytes 6148
  1162.2 94.4 %copy-start.35 = (f32[512]{0:T(512)S(1)}, f32[512]{0:T(512)}, u32[]{:S(2)}) copy-start(f32[512]{0:T(512)} %copy-done.34) | copy-start | bytes 6148
  1162.2 94.4 %copy-start.31 = (f32[512]{0:T(512)S(1)}, f32[512]{0:T(512)}, u32[]{:S(2)}) copy-start(f32[512]{0:T(512)} %copy-done.30) | copy-start | bytes 6148
  1257.4 43.5 %copy-start.1 = (bf16[768,768]{1,0:T(8,128)(2,1)S(1)}, bf16[768,768]{1,0:T(8,128)(2,1)}, u32[]{:S(2)}) copy-start(bf16[768,768]{1,0:T(8,128)(2,1)} %param.43) | copy-start | bytes 3538948
  (43 other events, 60.4 us)
Sparse Core Ops, SparseCore 0:
  13.7 65.5 all-gather.4
  195.8 109.4 reduce-scatter.4
  309.5 63.9 all-gather.6
  375.5 62.1 all-gather.8
  456.5 109.4 reduce-scatter.8
  568.2 111.2 reduce-scatter.6
  686.1 63.9 all-gather.10
  909.6 112.0 all-reduce.7
  1028.2 113.3 all-reduce.5
  1143.7 110.7 reduce-scatter.10
where the time goes:
time: 1320 us; the launch traced here: 1310 us
  waiting for transfers between devices  852 us (65%)
  local copies, waits for them, and re-layouts  216 us (16%)
  matrix products  118 us (9%)
  other arithmetic  59.5 us (5%)
  blocking collectives  40.9 us (3%)
  between operations  16.2 us (1%)
    unnamed x12, waiting for transfers between devices  217 us
    reduce_scatter x1, waiting for transfers between devices, body(): lax.psum_scatter(jnp.dot(activation, w_proj, preferred_element_type=jnp.f...  110 us
    reduce_scatter x1, waiting for transfers between devices, body(): lax.psum_scatter(jnp.dot(context, w_out, preferred_element_type=jnp.float...  108 us
    reduce_scatter x1, waiting for transfers between devices, body(): lax.psum_scatter(jnp.einsum('tf,df->td', grad_pre, w_fc, preferred_elemen...  101 us
    reduce_scatter x1, waiting for transfers between devices, body(): lax.psum_scatter(jnp.einsum('tcn,dcn->td', grad_mixed, w_qkv, preferred_e...  89.7 us
    all_gather x1, waiting for transfers between devices, body(): lax.all_gather(normed_share.astype(jnp.bfloat16), 'tensor', axis=0, tiled...  65.5 us
    all_gather x1, waiting for transfers between devices, body(): lax.all_gather(normed_share_two.astype(jnp.bfloat16), 'tensor', axis=0, t...  60.6 us
    all_gather x1, waiting for transfers between devices, body(): lax.all_gather(grad_top.astype(jnp.bfloat16), 'tensor', axis=0, tiled=True)  56.7 us
  transfers between devices with their start and end apart: 10, of which 10 were waited for; matrix products, arithmetic and copies ran while one was open for 5% of the time, Pallas kernels for 0%

commit v1 on v0

v1 whole, which is shorter than its diff:
```python
import functools

import jax
import jax.numpy as jnp
from jax import lax
from jax.experimental import pallas as pl
from jax.experimental.pallas import tpu as pltpu
from jax.sharding import PartitionSpec as P

BF = jnp.bfloat16
F32 = jnp.float32
EPS = 1e-5
NEG = -1e30
LOG2E = 1.4426950408889634
MESH = pl.DeviceIdType.MESH
RING = 4
GROUP = 2 * RING


def dot(a, b, ca=1, cb=0):
    return lax.dot_general(a, b, (((ca,), (cb,)), ((), ())), preferred_element_type=F32)


def nt(a, b):
    return dot(a, b, 1, 1)


def tn(a, b):
    return dot(a, b, 0, 0)


def al(v, m):
    return pl.multiple_of(v, m)


class Ids:
    def __init__(self):
        self.n = 0

    def __call__(self, k):
        base = self.n
        self.n += k
        return base


SID = Ids()
S_LEN, S_BIAS, S_HID, S_OG, S_AS1 = SID(1), SID(3), SID(1), SID(1), SID(3)
S_ARA, S_ARB = SID(4), SID(4)
S_MS1, S_MRA, S_MRB, S_MP = SID(6), SID(12), SID(12), SID(6)
S_N1, S_PO, S_GA, S_DX, S_BO, S_GI = SID(1), SID(1), SID(1), SID(1), SID(1), SID(1)
S_GP, S_G1, S_G2, S_GZ = SID(8), SID(16), SID(16), SID(8)
S_FA, S_FB, S_FC = SID(6), SID(4), SID(6)
S_A1, S_A2, S_AZ = SID(6), SID(6), SID(4)
S_HA, S_HB, S_HC = SID(3), SID(2), SID(3)
S_SM = SID(5)
RID = Ids()
R_LEN, R_BIAS, R_HID, R_OG, R_AS1 = RID(1), RID(3), RID(1), RID(1), RID(2)
R_ARA, R_ARB = RID(4), RID(4)
R_MS1, R_MRA, R_MRB, R_MP = RID(6), RID(12), RID(12), RID(6)
R_N1, R_PO, R_GA, R_DX, R_BO, R_GI = RID(1), RID(1), RID(1), RID(1), RID(1), RID(1)
R_GP, R_G1, R_G2, R_GZ = RID(8), RID(16), RID(16), RID(6)
R_FA, R_FB, R_FC = RID(6), RID(4), RID(6)
R_A1, R_A2, R_AZ = RID(6), RID(6), RID(12)
R_HA, R_HB, R_HC = RID(3), RID(2), RID(3)
R_SM = RID(5)


def kernel(
    lens, bias, vecs, hid_in, og_in, wq, wo, wf, wp,
    bo_out, gi_out, gm_out, ga_out, small_out,
    lrecv, bfa, hid, og, n1, watt, wmlp, q, k, v, qt, kt, vt, do, dot_, ot, ctx,
    mid, n2, oacc, dn2, act, dpre, ga, ps, pr, ps2, pr2, bo, gi,
    lse, dqa, cmask, kh, vh, qh,
    prb, r1b, r2b, zb, fs, gatt, a1b, a2b, azb, fa, sb, srb,
    ss, rs, ls,
):
    D = hid_in.shape[1]
    R = hid_in.shape[0]
    T = 2 * R
    HC = D // 2
    BQ = 256
    NB = T // BQ
    dp = lax.axis_index("dp")
    z = lax.axis_index("tensor")
    base = (dp // GROUP) * GROUP
    chip = (dp - base) // 2
    c = dp % 2
    oc = 1 - c
    cy = chip // 2
    cx = chip % 2
    r = 3 * cy + cx - 2 * cx * cy

    def ring_dp(rr, core):
        y = rr // 2
        x = rr % 2 + y - 2 * (rr % 2) * y
        return base + (2 * y + x) * 2 + core

    r_up = (r + 1) % RING
    r_dn = (r + 3) % RING
    r_op = (r + 2) % RING
    dev_up = (ring_dp(r_up, c), z)
    dev_dn = (ring_dp(r_dn, c), z)
    dev_pair = (dp + 1 - 2 * c, z)
    dev_z = [None] + [(dp, (z + dz) % 4) for dz in (1, 2, 3)]
    z_x = z + 1 - 2 * (z % 2)
    dev_swap = (dp + 1 - 2 * c, z_x)
    keep = c == z % 2
    swap = c != z % 2
    own_c = z // 2 == c
    not_own = z // 2 != c
    zz_own = z % 2
    pending = {}

    def when(cond, fn):
        if cond is None:
            fn()
        else:
            pl.when(cond)(fn)

    def desc(src, dst, sid, rid, dev):
        return pltpu.make_async_remote_copy(
            src_ref=src, dst_ref=dst, send_sem=ss.at[sid], recv_sem=rs.at[rid],
            device_id=dev, device_id_type=MESH,
        )

    def send(src, dst, sid, rid, dev, late=None, cond=None):
        desc(src, dst, sid, rid, dev).start()
        if late is not None:
            pending[sid] = (late, cond)

    def wsend(ref, sid):
        desc(ref, ref, sid, 0, dev_pair).wait_send()

    def wrecv(ref, rid):
        desc(ref, ref, 0, rid, dev_pair).wait_recv()

    barrier = pltpu.get_barrier_semaphore()
    for dev in (dev_up, dev_dn, dev_pair, dev_z[1], dev_z[2], dev_z[3], dev_swap):
        pl.semaphore_signal(barrier, inc=1, device_id=dev, device_id_type=MESH)
    pl.semaphore_wait(barrier, 7)

    loc_n = [0]

    def local(src, dst, cond=None):
        i = loc_n[0]
        loc_n[0] += 1
        cp = lambda: pltpu.make_async_copy(src(), dst(), ls.at[i])
        when(cond, lambda: cp().start())
        return lambda: when(cond, lambda: cp().wait())

    when(swap, lambda: send(hid_in, hid, S_HID, R_HID, dev_swap, lambda: hid_in, swap))
    w_hid = local(lambda: hid_in, lambda: hid, keep)
    send(lens, lrecv, S_LEN, R_LEN, dev_pair, lambda: lens)
    for dz in (1, 2, 3):
        send(bias, bfa.at[z], S_BIAS + dz - 1, R_BIAS + dz - 1, dev_z[dz], lambda: bias)
    ZS = D // 4

    def att_rows(zz):
        return pl.ds(al(zz * ZS, 16), ZS)

    def att_s1():
        for dz in (1, 2, 3):
            dst = watt.at[r, att_rows(zz_own)]

            def from_q():
                send(wq.at[jnp.minimum(r, 2)], dst, S_AS1 + dz - 1, R_AS1 + zz_own, dev_z[dz])

            def from_o():
                send(wo, dst, S_AS1 + dz - 1, R_AS1 + zz_own, dev_z[dz])

            pl.when(r < 3)(from_q)
            pl.when(r == 3)(from_o)
            pending[S_AS1 + dz - 1] = (lambda: wo, own_c)

    pl.when(own_c)(att_s1)
    w_wq = local(lambda: wq, lambda: watt.at[pl.ds(0, 3), att_rows(zz_own)], own_c)
    w_wo = local(lambda: wo, lambda: watt.at[3, att_rows(zz_own)], own_c)
    when(swap, lambda: send(og_in, og, S_OG, R_OG, dev_swap, lambda: og_in, swap))
    w_og = local(lambda: og_in, lambda: og, keep)
    w_mlp0 = [local(lambda: wf, lambda: wmlp.at[0, z]), local(lambda: wp, lambda: wmlp.at[1, z])]
    bfa[z] = bias[...]

    def zsh(dz):
        return (z - dz + 4) % 4

    def mg_s1(m, dz):
        w = (wf, wp)[m]
        u = m * 3 + dz - 1
        send(w.at[r, c], wmlp.at[m, z, r, c], S_MS1 + u, R_MS1 + u, dev_z[dz], lambda: w.at[r, c])

    def mg_a(m, dz):
        u = m * 3 + dz - 1
        piece = wmlp.at[m, zsh(dz), r, c]
        wrecv(piece, R_MS1 + u)
        send(piece, piece, S_MRA + 2 * u, R_MRA + 2 * u, dev_up)
        send(piece, piece, S_MRA + 2 * u + 1, R_MRA + 2 * u + 1, dev_dn)

    def mg_b(m, dz):
        u = m * 3 + dz - 1
        zp = zsh(dz)
        wrecv(wmlp.at[m, zp, r_dn, c], R_MRA + 2 * u)
        lo = wmlp.at[m, zp, r_dn, c, pl.ds(0, 48)]
        send(lo, lo, S_MRB + 2 * u, R_MRB + 2 * u, dev_up)
        wrecv(wmlp.at[m, zp, r_up, c], R_MRA + 2 * u + 1)
        hi = wmlp.at[m, zp, r_up, c, pl.ds(48, 48)]
        send(hi, hi, S_MRB + 2 * u + 1, R_MRB + 2 * u + 1, dev_dn)

    def mg_p(m, dz):
        u = m * 3 + dz - 1
        zp = zsh(dz)
        wrecv(wmlp.at[m, zp, r_op, c, pl.ds(0, 48)], R_MRB + 2 * u)
        wrecv(wmlp.at[m, zp, r_op, c, pl.ds(48, 48)], R_MRB + 2 * u + 1)
        mine = wmlp.at[m, zp, :, c]
        send(mine, mine, S_MP + u, R_MP + u, dev_pair)

    def mg_done(m, dz):
        u = m * 3 + dz - 1
        zp = zsh(dz)
        wrecv(wmlp.at[m, zp, :, oc], R_MP + u)
        for s in (0, 1):
            wsend(wmlp.at[m, zp, r, c], S_MRA + 2 * u + s)
            wsend(wmlp.at[m, zp, r, c, pl.ds(0, 48)], S_MRB + 2 * u + s)
        wsend(wmlp.at[m, zp, :, c], S_MP + u)

    munits = [(0, 1), (1, 1), (0, 2), (1, 2), (0, 3), (1, 3)]

    def mg_round(j):
        if 0 <= j < 6:
            mg_a(*munits[j])
        if 0 <= j - 1 < 6:
            mg_b(*munits[j - 1])
        if 0 <= j - 2 < 6:
            mg_p(*munits[j - 2])

    w_hid()
    when(swap, lambda: wrecv(hid, R_HID))
    row0 = c * R
    half = ZS // 2

    def stats(x):
        mu = jnp.mean(x, axis=1, keepdims=True)
        cen = x - mu
        var = jnp.mean(cen * cen, axis=1, keepdims=True)
        rstd = lax.rsqrt(var + EPS)
        return cen * rstd, rstd

    LB = 64

    def ln1_body(i, _):
        rows = pl.ds(al(i * LB, LB), LB)
        n, _r = stats(hid[rows, :].astype(F32))
        out = n * vecs[0:1, :] + vecs[1:2, :]
        n1[pl.ds(al(row0 + i * LB, LB), LB), :] = out.astype(BF)
        return 0

    lax.fori_loop(0, R // LB, ln1_body, 0)
    mine_rows = pl.ds(al(row0, R), R)
    pair_rows = pl.ds(al(oc * R, R), R)
    send(n1.at[mine_rows], n1.at[mine_rows], S_N1, R_N1, dev_pair, lambda: n1.at[mine_rows])

    kk = lax.broadcasted_iota(jnp.int32, (BQ, BQ), 0)
    qq = lax.broadcasted_iota(jnp.int32, (BQ, BQ), 1)
    cmask[...] = jnp.where(kk <= qq, 0.0, NEG)

    needs = (z != 2 * c, z != 2 * c + 1)

    def need(zz):
        return needs[zz]

    def ar_a(zz):
        piece = watt.at[r, att_rows(zz)]
        wrecv(piece, R_AS1 + zz)
        send(piece, piece, S_ARA + 2 * zz, R_ARA + 2 * zz, dev_up, lambda: wo, need(zz))
        send(piece, piece, S_ARA + 2 * zz + 1, R_ARA + 2 * zz + 1, dev_dn, lambda: wo, need(zz))

    def ar_b(zz):
        wrecv(watt.at[r_dn, att_rows(zz)], R_ARA + 2 * zz)
        lo = watt.at[r_dn, pl.ds(al(zz * ZS, 16), half)]
        send(lo, lo, S_ARB + 2 * zz, R_ARB + 2 * zz, dev_up, lambda: watt.at[0, pl.ds(0, half)], need(zz))
        wrecv(watt.at[r_up, att_rows(zz)], R_ARA + 2 * zz + 1)
        hi = watt.at[r_up, pl.ds(al(zz * ZS + half, 16), half)]
        send(hi, hi, S_ARB + 2 * zz + 1, R_ARB + 2 * zz + 1, dev_dn, lambda: watt.at[0, pl.ds(0, half)], need(zz))

    def ar_c(zz):
        wrecv(watt.at[r_op, pl.ds(al(zz * ZS, 16), half)], R_ARB + 2 * zz)
        wrecv(watt.at[r_op, pl.ds(al(zz * ZS + half, 16), half)], R_ARB + 2 * zz + 1)

    for step in (ar_a, ar_b):
        for zz in (0, 1):
            when(need(zz), functools.partial(step, zz))
    for dz in (1, 2, 3):
        mg_s1(0, dz)
        mg_s1(1, dz)
    for zz in (0, 1):
        when(need(zz), functools.partial(ar_c, zz))
    w_wq()
    w_wo()
    for dz in (1, 2, 3):
        wrecv(bfa.at[zsh(dz)], R_BIAS + dz - 1)
    wrecv(lrecv, R_LEN)
    keepf = 1.0 - (c + z % 2 - 2 * c * (z % 2)).astype(F32)
    length = lens[0:1, 0:1] * keepf + lrecv[0:1, 0:1] * (1.0 - keepf)
    wrecv(n1.at[pair_rows], R_N1)

    bqv = bfa[2 * c, 1:2, :] + bfa[2 * c + 1, 1:2, :]

    def qkv_body(i, _):
        rows = pl.ds(al(i * BQ, BQ), BQ)
        x = n1[rows, :]
        q[rows, :] = (nt(x, watt[0]) + bqv[:, :HC]).astype(BF)
        k[rows, :] = nt(x, watt[1]).astype(BF)
        v[rows, :] = (nt(x, watt[2]) + bqv[:, HC:]).astype(BF)
        return 0

    lax.fori_loop(0, NB, qkv_body, 0)

    def tr_body(i, _):
        rows = pl.ds(al(i * BQ, BQ), BQ)
        for hp in range(3):
            lanes = slice(hp * 128, hp * 128 + 128)
            qt[lanes, rows] = q[rows, lanes].T
            kt[lanes, rows] = k[rows, lanes].T
            vt[lanes, rows] = v[rows, lanes].T
        return 0

    lax.fori_loop(0, NB, tr_body, 0)

    lane = lax.broadcasted_iota(jnp.int32, (1, 128), 1)
    sub = lax.broadcasted_iota(jnp.int32, (128, 1), 0)
    pos = lax.broadcasted_iota(jnp.int32, (T, 1), 0).astype(F32)
    keybias = jnp.where(pos < length, 0.0, NEG)
    CS = 0.125 * LOG2E

    def head_prep(hp, hh):
        lanes = pl.ds(al(hp * 128, 128), 128)
        inhead = (lane // 64) == hh
        aux = lane == (1 - hh) * 64
        kp = k[:, lanes].astype(F32)
        kh[...] = jnp.where(inhead, kp, jnp.where(aux, keybias, 0.0)).astype(BF)
        qp = qt[lanes, :].astype(F32)
        qh[...] = jnp.where(sub == (1 - hh) * 64, 1.0, qp).astype(BF)
        return lanes, inhead

    def fwd_head(h, _):
        hp = h // 2
        hh = h % 2
        head_prep(hp, hh)
        hrows = pl.ds(al(h * 64, 64), 64)
        for qb in range(NB):
            nk = (qb + 1) * BQ
            cols = slice(qb * BQ, nk)
            s = dot(kh[:nk, :], qh[:, cols])
            diag = s[nk - BQ :] + cmask[...]
            s = diag if qb == 0 else jnp.concatenate([s[: nk - BQ], diag], axis=0)
            m = jnp.max(s, axis=0, keepdims=True) * CS
            p = jnp.exp2(s * CS - m)
            l = jnp.sum(p, axis=0, keepdims=True)
            o = dot(vt[hrows, :nk], p.astype(BF)) * (1.0 / l)
            ot[hrows, cols] = o.astype(BF)
            lse[h, 0:1, cols] = m + jnp.log(l) * LOG2E
        for j in range(6):
            pl.when(h == j)(functools.partial(mg_round, j))
        return 0

    lax.fori_loop(0, 6, fwd_head, 0)

    def ctx_body(i, _):
        rows = pl.ds(al(i * BQ, BQ), BQ)
        for hp in range(3):
            lanes = slice(hp * 128, hp * 128 + 128)
            ctx[rows, lanes] = ot[lanes, rows].T
        return 0

    lax.fori_loop(0, NB, ctx_body, 0)
    mg_round(6)

    ps[...] = dot(ctx[pair_rows, :], watt[3]).astype(BF)
    send(ps, pr, S_PO, R_PO, dev_pair, lambda: ps)
    mid[...] = hid[...].astype(F32) + vecs[2:3, :] + dot(ctx[mine_rows, :], watt[3])
    w_og()
    when(swap, lambda: wrecv(og, R_OG))
    wrecv(pr, R_PO)

    sb[...] = jnp.zeros_like(sb)

    def ln2_body(i, _):
        rows = pl.ds(al(i * LB, LB), LB)
        x = mid[rows, :] + pr[rows, :].astype(F32)
        mid[rows, :] = x
        n, _r = stats(x)
        n2[rows, :] = (n * vecs[3:4, :] + vecs[4:5, :]).astype(BF)
        p0 = lax.broadcasted_iota(jnp.int32, (LB, 1), 0).astype(F32) + (row0 + i * LB).astype(F32)
        g = og[rows, :].astype(F32) * jnp.where(p0 < length, 1.0, 0.0)
        og[rows, :] = g.astype(BF)
        sb[5:6, :] += jnp.sum(g, axis=0, keepdims=True)
        oacc[rows, :] = jnp.zeros((LB, D), F32)
        dn2[rows, :] = jnp.zeros((LB, D), F32)
        return 0

    lax.fori_loop(0, R // LB, ln2_body, 0)
    for w in w_mlp0:
        w()

    def zdst(i):
        return (z - i + 4) % 4

    def blk(m, i):
        return wmlp.at[m, zdst(i)]

    def add_into(dst, *others):
        t = dst[...].astype(F32)
        for o in others:
            t = t + o[...].astype(F32)
        dst[...] = t.astype(BF)

    def g_s0(m, i):
        u = m * 4 + i
        send(blk(m, i).at[:, oc], prb.at[u], S_GP + u, R_GP + u, dev_pair, lambda: blk(m, i).at[:, oc])

    def g_s1(m, i):
        u = m * 4 + i
        g = blk(m, i)
        wrecv(prb.at[u], R_GP + u)
        add_into(g.at[:, c], prb.at[u])
        send(g.at[r_op, c, pl.ds(0, 48)], r1b.at[u, 0], S_G1 + 2 * u, R_G1 + 2 * u, dev_up,
             lambda: r1b.at[u, 0])
        send(g.at[r_op, c, pl.ds(48, 48)], r1b.at[u, 1], S_G1 + 2 * u + 1, R_G1 + 2 * u + 1, dev_dn,
             lambda: r1b.at[u, 1])

    def g_s2(m, i):
        u = m * 4 + i
        g = blk(m, i)
        wrecv(r1b.at[u, 0], R_G1 + 2 * u)
        add_into(g.at[r_up, c, pl.ds(0, 48)], r1b.at[u, 0])
        send(g.at[r_up, c], r2b.at[u, 0], S_G2 + 2 * u, R_G2 + 2 * u, dev_up, lambda: r2b.at[u, 0])
        wrecv(r1b.at[u, 1], R_G1 + 2 * u + 1)
        add_into(g.at[r_dn, c, pl.ds(48, 48)], r1b.at[u, 1])
        send(g.at[r_dn, c], r2b.at[u, 1], S_G2 + 2 * u + 1, R_G2 + 2 * u + 1, dev_dn, lambda: r2b.at[u, 1])

    def g_s3(m, i):
        u = m * 4 + i
        g = blk(m, i)
        wrecv(r2b.at[u, 0], R_G2 + 2 * u)
        wrecv(r2b.at[u, 1], R_G2 + 2 * u + 1)
        add_into(g.at[r, c], r2b.at[u, 0], r2b.at[u, 1])
        if i > 0:
            send(g.at[r, c], zb.at[m, i - 1], S_GZ + u, R_GZ + m * 3 + i - 1, (dp, zdst(i)),
                 lambda: zb.at[m, i - 1])

    def g_fin(m):
        for i in (1, 2, 3):
            wrecv(zb.at[m, i - 1], R_GZ + m * 3 + i - 1)
        t = wmlp[m, z, r, c].astype(F32)
        for i in range(3):
            t = t + zb[m, i].astype(F32)
        fs[m] = t.astype(BF)
        dst = gm_out.at[m, r, c]
        send(fs.at[m], dst, S_FA + 3 * m, R_FA + 3 * m, dev_up, lambda: fs.at[m])
        send(fs.at[m], dst, S_FA + 3 * m + 1, R_FA + 3 * m + 1, dev_dn, lambda: fs.at[m])
        send(fs.at[m], dst, S_FA + 3 * m + 2, R_FA + 3 * m + 2, dev_pair, lambda: fs.at[m])

    def g_ag(m):
        lo = gm_out.at[m, r_dn, c, pl.ds(0, 48)]
        hi = gm_out.at[m, r_up, c, pl.ds(48, 48)]
        wrecv(gm_out.at[m, r_dn, c], R_FA + 3 * m)
        send(lo, lo, S_FB + 2 * m, R_FB + 2 * m, dev_up, lambda: r1b.at[0, 0])
        full = gm_out.at[m, r_dn, c]
        send(full, full, S_FC + 3 * m, R_FC + 3 * m, dev_pair, lambda: fs.at[m])
        wrecv(gm_out.at[m, r_up, c], R_FA + 3 * m + 1)
        send(hi, hi, S_FB + 2 * m + 1, R_FB + 2 * m + 1, dev_dn, lambda: r1b.at[0, 0])
        full2 = gm_out.at[m, r_up, c]
        send(full2, full2, S_FC + 3 * m + 1, R_FC + 3 * m + 1, dev_pair, lambda: fs.at[m])

    def g_ag2(m):
        wrecv(gm_out.at[m, r_op, c, pl.ds(0, 48)], R_FB + 2 * m)
        wrecv(gm_out.at[m, r_op, c, pl.ds(48, 48)], R_FB + 2 * m + 1)
        full = gm_out.at[m, r_op, c]
        send(full, full, S_FC + 3 * m + 2, R_FC + 3 * m + 2, dev_pair, lambda: fs.at[m])

    def g_end(m):
        wrecv(gm_out.at[m, r, oc], R_FA + 3 * m + 2)
        wrecv(gm_out.at[m, r_dn, oc], R_FC + 3 * m)
        wrecv(gm_out.at[m, r_up, oc], R_FC + 3 * m + 1)
        wrecv(gm_out.at[m, r_op, oc], R_FC + 3 * m + 2)

    GA_ = 0.7978845608028654

    def mlp_body(i, _):
        zp = (z - i + 4) % 4

        def got(dz):
            mg_done(0, dz)
            mg_done(1, dz)

        for dz in (1, 2, 3):
            pl.when(i == dz)(functools.partial(got, dz))
        for fb in range(D // 256):
            cols = slice(fb * 256, fb * 256 + 256)
            fcb = wmlp[0, zp, :, :, :, cols].reshape(D, 256)
            pre = dot(n2[...], fcb) + bfa[zp, 0:1, cols]
            sq = pre * pre
            t = jnp.tanh(GA_ * (pre + 0.044715 * (pre * sq)))
            hf = 0.5 * (1.0 + t)
            act[:, cols] = (pre * hf).astype(BF)
            gp = hf + (0.5 * GA_) * pre * (1.0 - t * t) * (1.0 + 0.134145 * sq)
            prj = wmlp[1, zp].reshape(D, D)[cols, :]
            dp_ = (nt(og[...], prj) * gp).astype(BF)
            dpre[:, cols] = dp_
            sb[pl.ds(6 + zp, 1), cols] = jnp.sum(dp_.astype(F32), axis=0, keepdims=True)
        prj = wmlp[1, zp].reshape(D, D)
        fc = wmlp[0, zp].reshape(D, D)
        for rb in range(R // 256):
            rows = slice(rb * 256, rb * 256 + 256)
            oacc[rows, :] += dot(act[rows, :], prj)
            dn2[rows, :] += nt(dpre[rows, :], fc)
        for j in range(2):
            cols = slice(j * HC, j * HC + HC)
            wmlp[1, zp, 2 * j : 2 * j + 2] = tn(act[:, cols], og[...]).astype(BF).reshape(2, 2, D // 8, D)
        for j in range(2):
            cols = slice(j * HC, j * HC + HC)
            wmlp[0, zp, 2 * j : 2 * j + 2] = tn(n2[:, cols], dpre[...]).astype(BF).reshape(2, 2, D // 8, D)

        def after(kk_):
            if kk_ >= 1:
                for m in (1, 0):
                    g_s1(m, kk_ - 1)
            g_s0(1, kk_)
            g_s0(0, kk_)

        for kk_ in range(4):
            pl.when(i == kk_)(functools.partial(after, kk_))
        return 0

    mg_round(7)
    lax.fori_loop(0, 4, mlp_body, 0)

    def bwd2_body(i, _):
        rows = pl.ds(al(i * LB, LB), LB)
        x = mid[rows, :]
        p0 = lax.broadcasted_iota(jnp.int32, (LB, 1), 0).astype(F32) + (row0 + i * LB).astype(F32)
        ok = jnp.where(p0 < length, 1.0, 0.0)
        bo[rows, :] = ((x + oacc[rows, :] + vecs[5:6, :]) * ok).astype(BF)
        n, rstd = stats(x)
        dn = dn2[rows, :]
        e = dn * vecs[3:4, :]
        em = jnp.mean(e, axis=1, keepdims=True)
        en = jnp.mean(e * n, axis=1, keepdims=True)
        gm = og[rows, :].astype(F32) + (e - em - n * en) * rstd
        mid[rows, :] = gm
        ga[pl.ds(al(row0 + i * LB, LB), LB), :] = gm.astype(BF)
        sb[2:3, :] += jnp.sum(dn * n, axis=0, keepdims=True)
        sb[3:4, :] += jnp.sum(dn, axis=0, keepdims=True)
        sb[4:5, :] += jnp.sum(gm, axis=0, keepdims=True)
        return 0

    lax.fori_loop(0, R // LB, bwd2_body, 0)
    send(ga.at[mine_rows], ga.at[mine_rows], S_GA, R_GA, dev_pair, lambda: ga.at[mine_rows])
    when(swap, lambda: send(bo, bo_out, S_BO, R_BO, dev_swap, lambda: bo, swap))
    w_bo = local(lambda: bo, lambda: bo_out, keep)
    wrecv(ga.at[pair_rows], R_GA)

    def dctx_body(i, _):
        rows = pl.ds(al(i * BQ, BQ), BQ)
        d = nt(ga[rows, :], watt[3])
        do[rows, :] = d.astype(BF)
        for hp in range(3):
            lanes = slice(hp * 128, hp * 128 + 128)
            dot_[lanes, rows] = do[rows, lanes].T
        return 0

    lax.fori_loop(0, NB, dctx_body, 0)

    def a_s1(hp):
        g = gatt.at[hp]
        send(g.at[r_op, pl.ds(0, 64)], a1b.at[hp, 0], S_A1 + 2 * hp, R_A1 + 2 * hp, dev_up, lambda: a1b.at[hp, 0])
        send(g.at[r_op, pl.ds(64, 64)], a1b.at[hp, 1], S_A1 + 2 * hp + 1, R_A1 + 2 * hp + 1, dev_dn,
             lambda: a1b.at[hp, 1])

    def a_s2(hp):
        g = gatt.at[hp]
        wrecv(a1b.at[hp, 0], R_A1 + 2 * hp)
        add_into(g.at[r_up, pl.ds(0, 64)], a1b.at[hp, 0])
        send(g.at[r_up], a2b.at[hp, 0], S_A2 + 2 * hp, R_A2 + 2 * hp, dev_up, lambda: a2b.at[hp, 0])
        wrecv(a1b.at[hp, 1], R_A1 + 2 * hp + 1)
        add_into(g.at[r_dn, pl.ds(64, 64)], a1b.at[hp, 1])
        send(g.at[r_dn], a2b.at[hp, 1], S_A2 + 2 * hp + 1, R_A2 + 2 * hp + 1, dev_dn, lambda: a2b.at[hp, 1])

    parts = [(0, 0, 128, 0, 0), (1, 0, 64, 0, 128), (1, 64, 64, 1, 0), (2, 0, 128, 1, 64)]

    def a_s3(hp):
        g = gatt.at[hp]
        wrecv(a2b.at[hp, 0], R_A2 + 2 * hp)
        wrecv(a2b.at[hp, 1], R_A2 + 2 * hp + 1)
        add_into(g.at[r], a2b.at[hp, 0], a2b.at[hp, 1])
        for pi, (ph, lo, n, zz, to) in enumerate(parts):
            if ph != hp:
                continue

            def go(pi=pi, lo=lo, n=n, zz=zz, to=to):
                zd = 2 * c + zz
                slot = (zd - z + 3) % 4
                send(g.at[r, pl.ds(lo, n)], azb.at[slot, pl.ds(to, n)], S_AZ + pi,
                     R_AZ + 3 * pi + slot, (dp, zd), lambda: gatt.at[hp, 0, pl.ds(lo, n)], need(zz))

            pl.when(need(zz))(go)

    def a_fin(zz):
        for pi, (ph, lo, n, zo, to) in enumerate(parts):
            if zo != zz:
                continue
            for slot in range(3):
                wrecv(azb.at[slot, pl.ds(to, n)], R_AZ + 3 * pi + slot)
            t = gatt[ph, r, lo : lo + n].astype(F32)
            for slot in range(3):
                t = t + azb[slot, to : to + n].astype(F32)
            fa[to : to + n] = t.astype(BF)

    def a_ag():
        for i, dev in enumerate((dev_up, dev_dn, dev_pair)):
            send(fa, ga_out.at[r], S_HA + i, R_HA + i, dev, lambda: fa, own_c)

    def a_ag2():
        lo = ga_out.at[r_dn, pl.ds(0, half)]
        hi = ga_out.at[r_up, pl.ds(half, half)]
        wrecv(ga_out.at[r_dn], R_HA)
        send(lo, lo, S_HB, R_HB, dev_up, lambda: fa.at[pl.ds(0, half)], own_c)
        send(ga_out.at[r_dn], ga_out.at[r_dn], S_HC, R_HC, dev_pair, lambda: fa, own_c)
        wrecv(ga_out.at[r_up], R_HA + 1)
        send(hi, hi, S_HB + 1, R_HB + 1, dev_dn, lambda: fa.at[pl.ds(0, half)], own_c)
        send(ga_out.at[r_up], ga_out.at[r_up], S_HC + 1, R_HC + 1, dev_pair, lambda: fa, own_c)

    def a_ag3():
        wrecv(ga_out.at[r_op, pl.ds(0, half)], R_HB)
        wrecv(ga_out.at[r_op, pl.ds(half, half)], R_HB + 1)
        send(ga_out.at[r_op], ga_out.at[r_op], S_HC + 2, R_HC + 2, dev_pair, lambda: fa, own_c)

    def a_end():
        wrecv(ga_out.at[r], R_HA + 2)
        wrecv(ga_out.at[r_dn], R_HC)
        wrecv(ga_out.at[r_up], R_HC + 1)
        wrecv(ga_out.at[r_op], R_HC + 2)

    def bwd_head(hp, hh):
        h = hp * 2 + hh
        lanes, inhead = head_prep(hp, hh)
        hrows = pl.ds(al(h * 64, 64), 64)
        vh[...] = jnp.where(inhead, v[:, lanes].astype(F32), 0.0).astype(BF)
        dl = jnp.sum(dot_[hrows, :].astype(F32) * ot[hrows, :].astype(F32), axis=0, keepdims=True)
        ls_h = lse[h]
        for kb in range(NB):
            krows = slice(kb * BQ, kb * BQ + BQ)
            qs = slice(kb * BQ, T)
            s = dot(kh[krows, :], qh[:, qs])
            diag = s[:, :BQ] + cmask[...]
            s = diag if kb == NB - 1 else jnp.concatenate([diag, s[:, BQ:]], axis=1)
            p = jnp.exp2(s * CS - ls_h[0:1, qs])
            dpr = dot(vh[krows, :], dot_[lanes, qs])
            ds = (p * (dpr - dl[:, qs])).astype(BF)
            dv = dot(p.astype(BF), do[qs, lanes])
            dk = dot(ds, q[qs, lanes]) * 0.125
            v[krows, lanes] = jnp.where(inhead, dv, v[krows, lanes].astype(F32)).astype(BF)
            k[krows, lanes] = jnp.where(inhead, dk, k[krows, lanes].astype(F32)).astype(BF)
            piece = dot(kt[hrows, krows], ds)
            if kb == 0:
                dqa[...] = piece
            else:
                dqa[:, qs] += piece
        qt[hrows, :] = (dqa[...] * 0.125).astype(BF)

    def bwd_pair(hp, _):
        def head(hh, _):
            bwd_head(hp, hh)
            return 0

        lax.fori_loop(0, 2, head, 0)
        lanes = pl.ds(al(hp * 128, 128), 128)

        def tr2(i, _):
            rows = pl.ds(al(i * BQ, BQ), BQ)
            q[rows, lanes] = qt[lanes, rows].T
            kt[lanes, rows] = k[rows, lanes].T
            vt[lanes, rows] = v[rows, lanes].T
            return 0

        lax.fori_loop(0, NB, tr2, 0)
        for t, ref in enumerate((qt, kt, vt)):
            gatt[hp, t] = dot(ref[lanes, :], n1[...]).astype(BF)
        gatt[hp, 3] = dot(ot[lanes, :], ga[...]).astype(BF)
        for j in range(3):
            pl.when(hp == j)(functools.partial(after_pair, j))
        return 0

    def after_pair(j):
        if j == 0:
            for i in range(3):
                for m in (1, 0):
                    g_s2(m, i)
            for m in (1, 0):
                g_s1(m, 3)
            a_s1(0)
        if j == 1:
            for i in range(3):
                for m in (1, 0):
                    g_s3(m, i)
            for m in (1, 0):
                g_s2(m, 3)
            a_s2(0)
            a_s1(1)
        if j == 2:
            for m in (1, 0):
                g_s3(m, 3)
            a_s2(1)
            a_s1(2)
            a_s3(0)
            for m in (1, 0):
                g_fin(m)

    lax.fori_loop(0, 3, bwd_pair, 0)

    def dx(rows):
        return dot(q[rows, :], watt[0]) + dot(k[rows, :], watt[1]) + dot(v[rows, :], watt[2])

    ps2[...] = dx(pair_rows).astype(BF)
    send(ps2, pr2, S_DX, R_DX, dev_pair, lambda: ps2)
    a_s2(2)
    a_s3(1)
    for m in (1, 0):
        g_ag(m)
    dn2[...] = dx(mine_rows)
    a_s3(2)
    sb[pl.ds(10 + c, 1), :] = jnp.concatenate(
        [jnp.sum(q[...].astype(F32), axis=0, keepdims=True), jnp.sum(v[...].astype(F32), axis=0, keepdims=True)],
        axis=1,
    )
    wrecv(pr2, R_DX)

    def bwd1_body(i, _):
        rows = pl.ds(al(i * LB, LB), LB)
        n, rstd = stats(hid[rows, :].astype(F32))
        dn = dn2[rows, :] + pr2[rows, :].astype(F32)
        e = dn * vecs[0:1, :]
        em = jnp.mean(e, axis=1, keepdims=True)
        en = jnp.mean(e * n, axis=1, keepdims=True)
        gi[rows, :] = (mid[rows, :] + (e - em - n * en) * rstd).astype(BF)
        sb[0:1, :] += jnp.sum(dn * n, axis=0, keepdims=True)
        sb[1:2, :] += jnp.sum(dn, axis=0, keepdims=True)
        return 0

    lax.fori_loop(0, R // LB, bwd1_body, 0)
    when(swap, lambda: send(gi, gi_out, S_GI, R_GI, dev_swap, lambda: gi, swap))
    w_gi = local(lambda: gi, lambda: gi_out, keep)

    p_ra = (ring_dp(r + 1 - 2 * (r % 2), c), z)
    p_rb = (ring_dp((r + 3 + 2 * (r % 2)) % RING, c), z)
    stages = [dev_pair, p_ra, p_rb, (dp, z_x), dev_z[2]]

    def small_step(j):
        send(sb.at[pl.ds(16 * j, 16)], srb.at[j], S_SM + j, R_SM + j, stages[j], lambda: srb.at[j])

    def small_add(j):
        wrecv(srb.at[j], R_SM + j)
        t = sb[16 * j : 16 * j + 16] + srb[j]
        if j < 4:
            sb[16 * j + 16 : 16 * j + 32] = t
        else:
            small_out[...] = t

    small_step(0)
    for m in (1, 0):
        g_ag2(m)
    small_add(0)
    small_step(1)
    for zz in (0, 1):
        when(z == 2 * c + zz, functools.partial(a_fin, zz))
    when(own_c, a_ag)
    small_add(1)
    small_step(2)
    when(own_c, a_ag2)
    small_add(2)
    small_step(3)
    when(own_c, a_ag3)
    small_add(3)
    small_step(4)
    small_add(4)

    w_fs = [local(lambda: fs.at[0], lambda: gm_out.at[0, r, c]), local(lambda: fs.at[1], lambda: gm_out.at[1, r, c])]
    w_fa = local(lambda: fa, lambda: ga_out.at[r], own_c)
    w_bo()
    w_gi()
    for w in w_fs:
        w()
    w_fa()
    for m in (0, 1):
        g_end(m)
    when(not_own, a_end)
    when(swap, lambda: wrecv(bo_out, R_BO))
    when(swap, lambda: wrecv(gi_out, R_GI))
    for sid, (ref, cond) in pending.items():
        when(cond, lambda sid=sid, ref=ref: wsend(ref(), sid))


def body(
    hidden_in, lengths, ln1_gain, ln1_bias, w_qkv, b_query, b_value, w_out, b_out,
    ln2_gain, ln2_bias, w_fc, b_fc, w_proj, b_proj, out_grad,
):
    R, D = hidden_in.shape
    T, HC, ZS, EB = 2 * R, D // 2, D // 4, D // 8
    z = lax.axis_index("tensor")
    lens = jnp.broadcast_to(jnp.where(z // 2 == 0, lengths[0], lengths[1]).astype(F32), (8, 128))
    zero = jnp.zeros((ZS,), BF)
    odd = z % 2 == 1
    qv_row = jnp.concatenate(
        [
            jnp.where(odd, zero, b_query), jnp.where(odd, b_query, zero),
            jnp.where(odd, zero, b_value), jnp.where(odd, b_value, zero),
        ]
    )
    blank = jnp.zeros((D,), BF)
    bias = jnp.stack([b_fc, qv_row] + [blank] * 6).astype(F32)
    vecs = jnp.stack([ln1_gain, ln1_bias, b_out, ln2_gain, ln2_bias, b_proj, blank, blank]).astype(F32)
    wq = jnp.transpose(w_qkv, (1, 2, 0))
    wf = w_fc.reshape(4, 2, EB, D)
    wp = w_proj.reshape(4, 2, EB, D)
    vm = lambda *s: pltpu.VMEM(s, BF)
    vf = lambda *s: pltpu.VMEM(s, F32)
    scratch = [
        vf(8, 128), vf(4, 8, D), vm(R, D), vm(R, D), vm(T, D), vm(4, HC, D), vm(2, 4, 4, 2, EB, D),
        vm(T, HC), vm(T, HC), vm(T, HC), vm(HC, T), vm(HC, T), vm(HC, T),
        vm(T, HC), vm(HC, T), vm(HC, T), vm(T, HC),
        vf(R, D), vm(R, D), vf(R, D), vf(R, D), vm(R, D), vm(R, D), vm(T, D),
        vm(R, D), vm(R, D), vm(R, D), vm(R, D), vm(R, D), vm(R, D),
        vf(6, 1, T), vf(64, T), vf(256, 256), vm(T, 128), vm(T, 128), vm(128, T),
        vm(8, 4, EB, D), vm(8, 2, EB // 2, D), vm(8, 2, EB, D), vm(2, 3, EB, D), vm(2, EB, D),
        vm(3, 4, 128, D), vm(3, 2, 64, D), vm(3, 2, 128, D), vm(3, ZS, D), vm(ZS, D),
        vf(80, D), vf(5, 16, D),
        pltpu.SemaphoreType.DMA((SID.n,)), pltpu.SemaphoreType.DMA((RID.n,)), pltpu.SemaphoreType.DMA((12,)),
    ]
    anyspec = pl.BlockSpec(memory_space=pl.ANY)
    vspec = pl.BlockSpec(memory_space=pltpu.VMEM)
    block_out, grad_input, gm, gatt, small = pl.pallas_call(
        kernel,
        out_shape=(
            jax.ShapeDtypeStruct((R, D), BF),
            jax.ShapeDtypeStruct((R, D), BF),
            jax.ShapeDtypeStruct((2, 4, 2, EB, D), BF),
            jax.ShapeDtypeStruct((4, ZS, D), BF),
            jax.ShapeDtypeStruct((16, D), F32),
        ),
        in_specs=[vspec] * 3 + [anyspec] * 6,
        out_specs=(anyspec, anyspec, anyspec, anyspec, vspec),
        scratch_shapes=scratch,
        compiler_params=pltpu.CompilerParams(
            collective_id=0, has_side_effects=True, vmem_limit_bytes=64 * 1024 * 1024 - 65536
        ),
        name="layer",
    )(lens, bias, vecs, hidden_in, out_grad, wq, w_out, wf, wp)
    data_count = lax.axis_size("dp")
    gm = gm.astype(F32)
    gatt = gatt.astype(F32)
    if data_count > GROUP:
        groups = [list(range(s, data_count, GROUP)) for s in range(GROUP)]
        gm, gatt, small = (lax.psum(t, "dp", axis_index_groups=groups) for t in (gm, gatt, small))
    g_fc = gm[0].reshape(D, D)
    g_proj = gm[1].reshape(D, D)
    g_qkv = jnp.transpose(gatt[:3], (2, 0, 1))
    b_fc_g = lax.dynamic_index_in_dim(small, 6 + z, 0, keepdims=False)
    b_row = lax.dynamic_index_in_dim(small, 10 + z // 2, 0, keepdims=False)
    gbq = jnp.where(odd, b_row[ZS : 2 * ZS], b_row[:ZS])
    gbv = jnp.where(odd, b_row[3 * ZS :], b_row[2 * ZS : 3 * ZS])
    return (
        block_out, grad_input, small[0], small[1], g_qkv, gbq, gbv, gatt[3], small[4],
        small[2], small[3], g_fc, b_fc_g, g_proj, small[5],
    )


def solution(mesh):
    rows = P(("dp", "tensor"), None)
    in_specs = (
        rows, P("dp"), P(), P(), P(None, None, "tensor"), P("tensor"), P("tensor"), P("tensor", None),
        P(), P(), P(), P(None, "tensor"), P("tensor"), P("tensor", None), P(), rows,
    )
    out_specs = (
        rows, rows, P(), P(), P(None, None, "tensor"), P("tensor"), P("tensor"), P("tensor", None),
        P(), P(), P(), P(None, "tensor"), P("tensor"), P("tensor", None), P(),
    )
    return jax.shard_map(body, mesh=mesh, in_specs=in_specs, out_specs=out_specs, check_vma=False)
```

time: 1320 us -> 215 us (0.16)
  waiting for transfers between devices: 852 us -> 0 us
  local copies, waits for them, and re-layouts: 216 us -> 15.1 us
  Pallas kernels: 0 us -> 189 us
  matrix products: 118 us -> 0 us
  other arithmetic: 59.5 us -> 4.96 us
  blocking collectives: 40.9 us -> 0 us
  between operations: 16.2 us -> 2.02 us
    reduce_scatter x4 -> x0, waiting for transfers between devices: 410 us -> none  [the longest x1 110 us: body(): lax.psum_scatter(jnp.dot(activation, w_proj, preferred_element_type=jnp.f...]
    all_gather x4 -> x0, waiting for transfers between devices: 226 us -> none  [the longest x1 65.5 us: body(): lax.all_gather(normed_share.astype(jnp.bfloat16), 'tensor', axis=0, tiled...]
    unnamed x12 -> x0, waiting for transfers between devices: 217 us -> none
    pallas_call x0 -> x1, Pallas kernels: none -> 189 us  [body(): pl.pallas_call(kernel, out_shape=(jax.ShapeDtypeStruct((R, D), BF), jax.S...]
    dot_general x66 -> x0, matrix products: 110 us -> none  [the longest x1 12.5 us: body(): jnp.einsum('td,fd->tf', grad_mlp, w_proj, preferred_element_type=jnp.floa...]
    concatenate x1 -> x0, local copies, waits for them, and re-layouts: 52.6 us -> none  [flatten_grads(): return jnp.concatenate([flat_grads, jnp.zeros((padding,), jnp.float32)])]
    dynamic_update_slice x18 -> x0, local copies, waits for them, and re-layouts: 41.9 us -> none  [the longest x10 36 us: body(): lax.map(forward_one, (queries, key_rows, value_rows, lengths))]
    psum x1 -> x0, blocking collectives: 40.9 us -> none  [body(): lax.psum((grad_gain_one, grad_shift_one, grad_gain_two, grad_shift_two, j...]
  transfers between devices with their start and end apart: 10 -> 0, of which waited for: 10 -> 0; matrix products, arithmetic and copies ran while one was open for 5% -> 0% of each run, Pallas kernels for 0% -> 0%
where the time goes in v1:
time: 215 us; the launch traced here: 211 us
  Pallas kernels  189 us (88%)
  local copies, waits for them, and re-layouts  15.1 us (7%)
  other arithmetic  4.96 us (2%)
    pallas_call x1, Pallas kernels, body(): pl.pallas_call(kernel, out_shape=(jax.ShapeDtypeStruct((R, D), BF), jax.S...  189 us

profile of v1, /device:TPU:1, one launch (start us, length us, event | category | flops | bytes accessed | tf_op | source)
XLA Modules:
  0.0 211.4 jit_solution(17376795431805083382)
XLA Ops:
  0.7 0.1 pad.3.clone
  0.8 1.3 fusion.1
  3.4 0.7 broadcast_select_fusion.3
  4.1 0.1 pad_maximum_fusion
  4.1 0.7 stack.37
  4.8 0.7 stack.38
  5.5 0.7 stack.39
  6.2 0.7 stack.40
  6.9 0.7 stack.41
  7.6 0.7 stack.33
  8.3 0.7 stack.42
  9.0 0.6 broadcast_in_dim.6.lens
  9.6 0.6 convert_element_type.17.vecs
  10.2 0.7 maximum_convert_fusion.bias
  10.9 189.3 %layer.1 = (bf16[512,768]{1,0:T(8,128)(2,1)}, bf16[512,768]{1,0:T(8,128)(2,1)}, bf16[2,4,2,96,768]{4,3,2,1,0:T(8,128)(2,1)}, bf16[4,192,768]{2,1,0:T(8,128)(2,1)}, f32[16,768]{1,0:T(8,128)}) custom-call(f32[8,128]{1,0:T(8,128)} %broadcast_in_dim.6.lens, f32[8,768]{1,0:T(8,128)} %maximum_convert_fusion.bias, f32[8,768]{1,0:T(8,128)} %convert_element_type.17.vecs, ...), custom_call_target="tpu_custom_call" | custom-call | tf_op jit(solution)/shard_map/layer/pallas_call | solution.py:840
  200.2 1.4 broadcast_select_fusion
  201.6 1.7 slice_reduce_fusion
  203.3 1.5 convert_element_type.18
  204.7 0.0 copy-start
  204.8 0.9 slice_bitcast_fusion.1
  205.6 1.3 slice_bitcast_fusion
  206.9 0.0 copy-done
  206.9 0.0 copy-start.2
  206.9 0.0 copy-start.1
  206.9 2.7 %fusion = (f32[1,4,2,96,768]{4,3,2,1,0:T(8,128)}, f32[1,4,2,96,768]{4,3,2,1,0:T(8,128)}) fusion(bf16[2,4,2,96,768]{4,3,2,1,0:T(8,128)(2,1)S(1)} %copy-done), kind=kLoop, calls=%fused_computation.17 | loop fusion | bytes 9437184 | tf_op jit(solution)/shard_map/slice | solution.py:864
  209.6 0.0 copy-done.2
  209.6 0.9 copy.33
  210.5 0.0 copy-done.1
  210.5 0.9 copy.34
  (4 shorter events, 0.1 us)
Async XLA Ops:
  204.7 2.2 %copy-start = (bf16[2,4,2,96,768]{4,3,2,1,0:T(8,128)(2,1)S(1)}, bf16[2,4,2,96,768]{4,3,2,1,0:T(8,128)(2,1)}, u32[]{:S(2)}) copy-start(bf16[2,4,2,96,768]{4,3,2,1,0:T(8,128)(2,1)} %get-tuple-element.24) | copy-start | bytes 7077892
  206.9 2.7 %copy-start.2 = (bf16[512,768]{1,0:T(8,128)(2,1)S(1)}, bf16[512,768]{1,0:T(8,128)(2,1)}, u32[]{:S(2)}) copy-start(bf16[512,768]{1,0:T(8,128)(2,1)} %get-tuple-element.59) | copy-start | bytes 2359300
  206.9 3.6 %copy-start.1 = (bf16[512,768]{1,0:T(8,128)(2,1)S(1)}, bf16[512,768]{1,0:T(8,128)(2,1)}, u32[]{:S(2)}) copy-start(bf16[512,768]{1,0:T(8,128)(2,1)} %get-tuple-element.60) | copy-start | bytes 2359300

commit v2 on v1

--- a/solution.py
+++ b/solution.py
@@ -17,6 +17,23 @@
 GROUP = 2 * RING
 
 
+T_LOOP = (("", "10"), ("11 20", "12"), ("13 21", "14"), ("15 22", "16"))
+T_BWD2 = "17 23 30"
+T_DCTX = "31"
+T_ATT = (("24", "32", "25", "33"), ("26", "34", "27", "35"), ("28", "36", "29", "37"))
+T_PAIR = ("18", "19", "110")
+T_DX = "38"
+T_DX2 = "210 39"
+T_LAST = "310"
+G_EARLY = ""
+G_QKV = "a0"
+G_TR = ""
+G_ATT = (("a1", "", "b0", ""), ("b1 a2", "", "p0 a3", "p1"), ("b2", "", "b3 p2", "a4"))
+G_CTX = ""
+G_MLP = "p3 a5"
+G_LOOP = (("b4", "b5"), ("p4", "p5"), ("", ""), ("", ""))
+
+
 def dot(a, b, ca=1, cb=0):
     return lax.dot_general(a, b, (((ca,), (cb,)), ((), ())), preferred_element_type=F32)
 
@@ -47,28 +64,28 @@
 S_LEN, S_BIAS, S_HID, S_OG, S_AS1 = SID(1), SID(3), SID(1), SID(1), SID(3)
 S_ARA, S_ARB = SID(4), SID(4)
 S_MS1, S_MRA, S_MRB, S_MP = SID(6), SID(12), SID(12), SID(6)
-S_N1, S_PO, S_GA, S_DX, S_BO, S_GI = SID(1), SID(1), SID(1), SID(1), SID(1), SID(1)
+S_N1, S_PO, S_GA, S_DX, S_BO, S_GI = SID(1), SID(1), SID(1), SID(1), SID(1), SID(8)
 S_GP, S_G1, S_G2, S_GZ = SID(8), SID(16), SID(16), SID(8)
 S_FA, S_FB, S_FC = SID(6), SID(4), SID(6)
 S_A1, S_A2, S_AZ = SID(6), SID(6), SID(4)
 S_HA, S_HB, S_HC = SID(3), SID(2), SID(3)
-S_SM = SID(5)
+S_SM = SID(7)
 RID = Ids()
 R_LEN, R_BIAS, R_HID, R_OG, R_AS1 = RID(1), RID(3), RID(1), RID(1), RID(2)
 R_ARA, R_ARB = RID(4), RID(4)
 R_MS1, R_MRA, R_MRB, R_MP = RID(6), RID(12), RID(12), RID(6)
-R_N1, R_PO, R_GA, R_DX, R_BO, R_GI = RID(1), RID(1), RID(1), RID(1), RID(1), RID(1)
+R_N1, R_PO, R_GA, R_DX, R_BO, R_GI = RID(1), RID(1), RID(1), RID(1), RID(1), RID(8)
 R_GP, R_G1, R_G2, R_GZ = RID(8), RID(16), RID(16), RID(6)
 R_FA, R_FB, R_FC = RID(6), RID(4), RID(6)
 R_A1, R_A2, R_AZ = RID(6), RID(6), RID(12)
 R_HA, R_HB, R_HC = RID(3), RID(2), RID(3)
-R_SM = RID(5)
+R_SM = RID(9)
 
 
 def kernel(
-    lens, bias, vecs, hid_in, og_in, wq, wo, wf, wp,
+    lengths, vecs, hid_in, og_in, wq, wo, wf, wp,
     bo_out, gi_out, gm_out, ga_out, small_out,
-    lrecv, bfa, hid, og, n1, watt, wmlp, q, k, v, qt, kt, vt, do, dot_, ot, ctx,
+    lens, lrecv, bfa, hid, og, n1, watt, wmlp, q, k, v, qt, kt, vt, do, dot_, ot, ctx,
     mid, n2, oacc, dn2, act, dpre, ga, ps, pr, ps2, pr2, bo, gi,
     lse, dqa, cmask, kh, vh, qh,
     prb, r1b, r2b, zb, fs, gatt, a1b, a2b, azb, fa, sb, srb,
@@ -100,6 +117,7 @@
     r_op = (r + 2) % RING
     dev_up = (ring_dp(r_up, c), z)
     dev_dn = (ring_dp(r_dn, c), z)
+    dev_op = (ring_dp(r_op, c), z)
     dev_pair = (dp + 1 - 2 * c, z)
     dev_z = [None] + [(dp, (z + dz) % 4) for dz in (1, 2, 3)]
     z_x = z + 1 - 2 * (z % 2)
@@ -135,9 +153,9 @@
         desc(ref, ref, 0, rid, dev_pair).wait_recv()
 
     barrier = pltpu.get_barrier_semaphore()
-    for dev in (dev_up, dev_dn, dev_pair, dev_z[1], dev_z[2], dev_z[3], dev_swap):
+    cross = [(dp + 1 - 2 * c, (z + dz) % 4) for dz in (1, 2, 3)]
+    for dev in (dev_up, dev_dn, dev_op, dev_pair, dev_z[1], dev_z[2], dev_z[3], *cross):
         pl.semaphore_signal(barrier, inc=1, device_id=dev, device_id_type=MESH)
-    pl.semaphore_wait(barrier, 7)
 
     loc_n = [0]
 
@@ -148,11 +166,8 @@
         when(cond, lambda: cp().start())
         return lambda: when(cond, lambda: cp().wait())
 
-    when(swap, lambda: send(hid_in, hid, S_HID, R_HID, dev_swap, lambda: hid_in, swap))
     w_hid = local(lambda: hid_in, lambda: hid, keep)
-    send(lens, lrecv, S_LEN, R_LEN, dev_pair, lambda: lens)
-    for dz in (1, 2, 3):
-        send(bias, bfa.at[z], S_BIAS + dz - 1, R_BIAS + dz - 1, dev_z[dz], lambda: bias)
+    bias = vecs.at[pl.ds(8, 8)]
     ZS = D // 4
 
     def att_rows(zz):
@@ -162,24 +177,22 @@
         for dz in (1, 2, 3):
             dst = watt.at[r, att_rows(zz_own)]
 
+            dev = (dp - c + z // 2, (z + dz) % 4)
+
             def from_q():
-                send(wq.at[jnp.minimum(r, 2)], dst, S_AS1 + dz - 1, R_AS1 + zz_own, dev_z[dz])
+                send(wq.at[jnp.minimum(r, 2)], dst, S_AS1 + dz - 1, R_AS1 + zz_own, dev)
 
             def from_o():
-                send(wo, dst, S_AS1 + dz - 1, R_AS1 + zz_own, dev_z[dz])
+                send(wo, dst, S_AS1 + dz - 1, R_AS1 + zz_own, dev)
 
             pl.when(r < 3)(from_q)
             pl.when(r == 3)(from_o)
-            pending[S_AS1 + dz - 1] = (lambda: wo, own_c)
-
-    pl.when(own_c)(att_s1)
+            pending[S_AS1 + dz - 1] = (lambda: wo, swap)
+
     w_wq = local(lambda: wq, lambda: watt.at[pl.ds(0, 3), att_rows(zz_own)], own_c)
     w_wo = local(lambda: wo, lambda: watt.at[3, att_rows(zz_own)], own_c)
-    when(swap, lambda: send(og_in, og, S_OG, R_OG, dev_swap, lambda: og_in, swap))
     w_og = local(lambda: og_in, lambda: og, keep)
     w_mlp0 = [local(lambda: wf, lambda: wmlp.at[0, z]), local(lambda: wp, lambda: wmlp.at[1, z])]
-    bfa[z] = bias[...]
-
     def zsh(dz):
         return (z - dz + 4) % 4
 
@@ -222,18 +235,12 @@
             wsend(wmlp.at[m, zp, r, c, pl.ds(0, 48)], S_MRB + 2 * u + s)
         wsend(wmlp.at[m, zp, :, c], S_MP + u)
 
-    munits = [(0, 1), (1, 1), (0, 2), (1, 2), (0, 3), (1, 3)]
-
-    def mg_round(j):
-        if 0 <= j < 6:
-            mg_a(*munits[j])
-        if 0 <= j - 1 < 6:
-            mg_b(*munits[j - 1])
-        if 0 <= j - 2 < 6:
-            mg_p(*munits[j - 2])
-
-    w_hid()
-    when(swap, lambda: wrecv(hid, R_HID))
+    munits = [(0, 1), (1, 1), (0, 3), (1, 3), (0, 2), (1, 2)]
+
+    def mg(steps):
+        for st in steps.split():
+            {"a": mg_a, "b": mg_b, "p": mg_p}[st[0]](*munits[int(st[1])])
+
     row0 = c * R
     half = ZS // 2
 
@@ -244,7 +251,7 @@
         rstd = lax.rsqrt(var + EPS)
         return cen * rstd, rstd
 
-    LB = 64
+    LB = 128
 
     def ln1_body(i, _):
         rows = pl.ds(al(i * LB, LB), LB)
@@ -253,14 +260,35 @@
         n1[pl.ds(al(row0 + i * LB, LB), LB), :] = out.astype(BF)
         return 0
 
-    lax.fori_loop(0, R // LB, ln1_body, 0)
     mine_rows = pl.ds(al(row0, R), R)
     pair_rows = pl.ds(al(oc * R, R), R)
-    send(n1.at[mine_rows], n1.at[mine_rows], S_N1, R_N1, dev_pair, lambda: n1.at[mine_rows])
+
+    def norm_one():
+        lax.fori_loop(0, R // LB, ln1_body, 0)
+
+    def norm_one_send():
+        send(n1.at[mine_rows], n1.at[mine_rows], S_N1, R_N1, dev_pair, lambda: n1.at[mine_rows])
+
+    def norm_one_far():
+        wrecv(hid, R_HID)
+        norm_one()
+        norm_one_send()
+
+    bfa[z] = bias[...]
+    w_hid()
+    pl.when(keep)(norm_one)
 
     kk = lax.broadcasted_iota(jnp.int32, (BQ, BQ), 0)
     qq = lax.broadcasted_iota(jnp.int32, (BQ, BQ), 1)
     cmask[...] = jnp.where(kk <= qq, 0.0, NEG)
+    pl.semaphore_wait(barrier, 10)
+    pl.when(swap)(att_s1)
+    when(swap, lambda: send(hid_in, hid, S_HID, R_HID, dev_swap, lambda: hid_in, swap))
+    for dz in (1, 2, 3):
+        send(bias, bfa.at[z], S_BIAS + dz - 1, R_BIAS + dz - 1, dev_z[dz], lambda: bias)
+    lens[...] = jnp.full((8, 128), lengths[z // 2].astype(F32))
+    send(lens, lrecv, S_LEN, R_LEN, dev_pair, lambda: lens)
+    pl.when(keep)(norm_one_send)
 
     needs = (z != 2 * c, z != 2 * c + 1)
 
@@ -285,12 +313,18 @@
         wrecv(watt.at[r_op, pl.ds(al(zz * ZS, 16), half)], R_ARB + 2 * zz)
         wrecv(watt.at[r_op, pl.ds(al(zz * ZS + half, 16), half)], R_ARB + 2 * zz + 1)
 
-    for step in (ar_a, ar_b):
-        for zz in (0, 1):
-            when(need(zz), functools.partial(step, zz))
-    for dz in (1, 2, 3):
+    for zz in (0, 1):
+        when(need(zz), functools.partial(ar_a, zz))
+    for dz in (1, 3):
         mg_s1(0, dz)
         mg_s1(1, dz)
+    for zz in (0, 1):
+        when(need(zz), functools.partial(ar_b, zz))
+    pl.when(swap)(norm_one_far)
+    mg_s1(0, 2)
+    mg_s1(1, 2)
+    when(swap, lambda: send(og_in, og, S_OG, R_OG, dev_swap, lambda: og_in, swap))
+    mg(G_EARLY)
     for zz in (0, 1):
         when(need(zz), functools.partial(ar_c, zz))
     w_wq()
@@ -313,6 +347,7 @@
         return 0
 
     lax.fori_loop(0, NB, qkv_body, 0)
+    mg(G_QKV)
 
     def tr_body(i, _):
         rows = pl.ds(al(i * BQ, BQ), BQ)
@@ -324,6 +359,7 @@
         return 0
 
     lax.fori_loop(0, NB, tr_body, 0)
+    mg(G_TR)
 
     lane = lax.broadcasted_iota(jnp.int32, (1, 128), 1)
     sub = lax.broadcasted_iota(jnp.int32, (128, 1), 0)
@@ -336,33 +372,38 @@
         inhead = (lane // 64) == hh
         aux = lane == (1 - hh) * 64
         kp = k[:, lanes].astype(F32)
-        kh[...] = jnp.where(inhead, kp, jnp.where(aux, keybias, 0.0)).astype(BF)
+        kh[hh] = jnp.where(inhead, kp, jnp.where(aux, keybias, 0.0)).astype(BF)
         qp = qt[lanes, :].astype(F32)
-        qh[...] = jnp.where(sub == (1 - hh) * 64, 1.0, qp).astype(BF)
+        qh[hh] = jnp.where(sub == (1 - hh) * 64, 1.0, qp).astype(BF)
         return lanes, inhead
 
-    def fwd_head(h, _):
-        hp = h // 2
-        hh = h % 2
-        head_prep(hp, hh)
-        hrows = pl.ds(al(h * 64, 64), 64)
+    def by_pair(hp, run, steps):
+        for j in range(3):
+            if steps[j]:
+                pl.when(hp == j)(functools.partial(run, steps[j]))
+
+    def fwd_pair(hp, _):
+        for hh in (0, 1):
+            head_prep(hp, hh)
         for qb in range(NB):
             nk = (qb + 1) * BQ
             cols = slice(qb * BQ, nk)
-            s = dot(kh[:nk, :], qh[:, cols])
-            diag = s[nk - BQ :] + cmask[...]
-            s = diag if qb == 0 else jnp.concatenate([s[: nk - BQ], diag], axis=0)
-            m = jnp.max(s, axis=0, keepdims=True) * CS
-            p = jnp.exp2(s * CS - m)
-            l = jnp.sum(p, axis=0, keepdims=True)
-            o = dot(vt[hrows, :nk], p.astype(BF)) * (1.0 / l)
-            ot[hrows, cols] = o.astype(BF)
-            lse[h, 0:1, cols] = m + jnp.log(l) * LOG2E
-        for j in range(6):
-            pl.when(h == j)(functools.partial(mg_round, j))
-        return 0
-
-    lax.fori_loop(0, 6, fwd_head, 0)
+            for hh in (0, 1):
+                h = hp * 2 + hh
+                hrows = pl.ds(al(h * 64, 64), 64)
+                s = dot(kh[hh, :nk, :], qh[hh, :, cols])
+                diag = s[nk - BQ :] + cmask[...]
+                s = diag if qb == 0 else jnp.concatenate([s[: nk - BQ], diag], axis=0)
+                m = jnp.max(s, axis=0, keepdims=True) * CS
+                p = jnp.exp2(s * CS - m)
+                l = jnp.sum(p, axis=0, keepdims=True)
+                o = dot(vt[hrows, :nk], p.astype(BF)) * (1.0 / l)
+                ot[hrows, cols] = o.astype(BF)
+                lse[h, 0:1, cols] = m + jnp.log(l) * LOG2E
+            by_pair(hp, mg, [G_ATT[j][qb] for j in range(3)])
+        return 0
+
+    lax.fori_loop(0, 3, fwd_pair, 0)
 
     def ctx_body(i, _):
         rows = pl.ds(al(i * BQ, BQ), BQ)
@@ -372,7 +413,7 @@
         return 0
 
     lax.fori_loop(0, NB, ctx_body, 0)
-    mg_round(6)
+    mg(G_CTX)
 
     ps[...] = dot(ctx[pair_rows, :], watt[3]).astype(BF)
     send(ps, pr, S_PO, R_PO, dev_pair, lambda: ps)
@@ -402,7 +443,7 @@
         w()
 
     def zdst(i):
-        return (z - i + 4) % 4
+        return (z - i - (i // 2) * (1 - 2 * (i % 2)) + 4) % 4
 
     def blk(m, i):
         return wmlp.at[m, zdst(i)]
@@ -483,17 +524,95 @@
         wrecv(gm_out.at[m, r_up, oc], R_FC + 3 * m + 1)
         wrecv(gm_out.at[m, r_op, oc], R_FC + 3 * m + 2)
 
+    def a_s1(hp):
+        g = gatt.at[hp]
+        send(g.at[r_op, pl.ds(0, 64)], a1b.at[hp, 0], S_A1 + 2 * hp, R_A1 + 2 * hp, dev_up, lambda: a1b.at[hp, 0])
+        send(g.at[r_op, pl.ds(64, 64)], a1b.at[hp, 1], S_A1 + 2 * hp + 1, R_A1 + 2 * hp + 1, dev_dn,
+             lambda: a1b.at[hp, 1])
+
+    def a_s2(hp):
+        g = gatt.at[hp]
+        wrecv(a1b.at[hp, 0], R_A1 + 2 * hp)
+        add_into(g.at[r_up, pl.ds(0, 64)], a1b.at[hp, 0])
+        send(g.at[r_up], a2b.at[hp, 0], S_A2 + 2 * hp, R_A2 + 2 * hp, dev_up, lambda: a2b.at[hp, 0])
+        wrecv(a1b.at[hp, 1], R_A1 + 2 * hp + 1)
+        add_into(g.at[r_dn, pl.ds(64, 64)], a1b.at[hp, 1])
+        send(g.at[r_dn], a2b.at[hp, 1], S_A2 + 2 * hp + 1, R_A2 + 2 * hp + 1, dev_dn, lambda: a2b.at[hp, 1])
+
+    parts = [(0, 0, 128, 0, 0), (1, 0, 64, 0, 128), (1, 64, 64, 1, 0), (2, 0, 128, 1, 64)]
+
+    def a_s3(hp):
+        g = gatt.at[hp]
+        wrecv(a2b.at[hp, 0], R_A2 + 2 * hp)
+        wrecv(a2b.at[hp, 1], R_A2 + 2 * hp + 1)
+        add_into(g.at[r], a2b.at[hp, 0], a2b.at[hp, 1])
+        for pi, (ph, lo, n, zz, to) in enumerate(parts):
+            if ph != hp:
+                continue
+
+            def go(pi=pi, lo=lo, n=n, zz=zz, to=to):
+                zd = 2 * c + zz
+                slot = (zd - z + 3) % 4
+                send(g.at[r, pl.ds(lo, n)], azb.at[slot, pl.ds(to, n)], S_AZ + pi,
+                     R_AZ + 3 * pi + slot, (dp, zd), lambda: gatt.at[hp, 0, pl.ds(lo, n)], need(zz))
+
+            pl.when(need(zz))(go)
+
+    def a_fin(zz):
+        for pi, (ph, lo, n, zo, to) in enumerate(parts):
+            if zo != zz:
+                continue
+            for slot in range(3):
+                wrecv(azb.at[slot, pl.ds(to, n)], R_AZ + 3 * pi + slot)
+            t = gatt[ph, r, lo : lo + n].astype(F32)
+            for slot in range(3):
+                t = t + azb[slot, to : to + n].astype(F32)
+            fa[to : to + n] = t.astype(BF)
+
+    def a_ag():
+        for i, dev in enumerate((dev_up, dev_dn, dev_pair)):
+            send(fa, ga_out.at[r], S_HA + i, R_HA + i, dev, lambda: fa, own_c)
+
+    def a_ag2():
+        lo = ga_out.at[r_dn, pl.ds(0, half)]
+        hi = ga_out.at[r_up, pl.ds(half, half)]
+        wrecv(ga_out.at[r_dn], R_HA)
+        send(lo, lo, S_HB, R_HB, dev_up, lambda: fa.at[pl.ds(0, half)], own_c)
+        send(ga_out.at[r_dn], ga_out.at[r_dn], S_HC, R_HC, dev_pair, lambda: fa, own_c)
+        wrecv(ga_out.at[r_up], R_HA + 1)
+        send(hi, hi, S_HB + 1, R_HB + 1, dev_dn, lambda: fa.at[pl.ds(0, half)], own_c)
+        send(ga_out.at[r_up], ga_out.at[r_up], S_HC + 1, R_HC + 1, dev_pair, lambda: fa, own_c)
+
+    def a_ag3():
+        wrecv(ga_out.at[r_op, pl.ds(0, half)], R_HB)
+        wrecv(ga_out.at[r_op, pl.ds(half, half)], R_HB + 1)
+        send(ga_out.at[r_op], ga_out.at[r_op], S_HC + 2, R_HC + 2, dev_pair, lambda: fa, own_c)
+
+    def a_end():
+        wrecv(ga_out.at[r], R_HA + 2)
+        wrecv(ga_out.at[r_dn], R_HC)
+        wrecv(ga_out.at[r_up], R_HC + 1)
+        wrecv(ga_out.at[r_op], R_HC + 2)
+
     GA_ = 0.7978845608028654
 
+    def gr(steps):
+        for st in steps.split():
+            kind, u = int(st[0]), int(st[1:])
+            if u < 8:
+                (g_s1, g_s2, g_s3)[kind - 1](1 - u % 2, u // 2)
+            else:
+                (a_s1, a_s2, a_s3)[kind - 1](u - 8)
+
     def mlp_body(i, _):
-        zp = (z - i + 4) % 4
+        zp = zdst(i)
 
         def got(dz):
             mg_done(0, dz)
             mg_done(1, dz)
 
-        for dz in (1, 2, 3):
-            pl.when(i == dz)(functools.partial(got, dz))
+        for it, dz in ((1, 1), (2, 3), (3, 2)):
+            pl.when(i == it)(functools.partial(got, dz))
         for fb in range(D // 256):
             cols = slice(fb * 256, fb * 256 + 256)
             fcb = wmlp[0, zp, :, :, :, cols].reshape(D, 256)
@@ -508,30 +627,33 @@
             dpre[:, cols] = dp_
             sb[pl.ds(6 + zp, 1), cols] = jnp.sum(dp_.astype(F32), axis=0, keepdims=True)
         prj = wmlp[1, zp].reshape(D, D)
+        for rb in range(R // 256):
+            rows = slice(rb * 256, rb * 256 + 256)
+            oacc[rows, :] += dot(act[rows, :], prj)
+        for j in range(2):
+            cols = slice(j * HC, j * HC + HC)
+            wmlp[1, zp, 2 * j : 2 * j + 2] = tn(act[:, cols], og[...]).astype(BF).reshape(2, 2, D // 8, D)
+        at(i, 0)
         fc = wmlp[0, zp].reshape(D, D)
         for rb in range(R // 256):
             rows = slice(rb * 256, rb * 256 + 256)
-            oacc[rows, :] += dot(act[rows, :], prj)
             dn2[rows, :] += nt(dpre[rows, :], fc)
         for j in range(2):
             cols = slice(j * HC, j * HC + HC)
-            wmlp[1, zp, 2 * j : 2 * j + 2] = tn(act[:, cols], og[...]).astype(BF).reshape(2, 2, D // 8, D)
-        for j in range(2):
-            cols = slice(j * HC, j * HC + HC)
             wmlp[0, zp, 2 * j : 2 * j + 2] = tn(n2[:, cols], dpre[...]).astype(BF).reshape(2, 2, D // 8, D)
-
-        def after(kk_):
-            if kk_ >= 1:
-                for m in (1, 0):
-                    g_s1(m, kk_ - 1)
-            g_s0(1, kk_)
-            g_s0(0, kk_)
-
+        at(i, 1)
+        return 0
+
+    def at(i, where):
         for kk_ in range(4):
-            pl.when(i == kk_)(functools.partial(after, kk_))
-        return 0
-
-    mg_round(7)
+            def here(kk_=kk_):
+                g_s0(1 - where, kk_)
+                mg(G_LOOP[kk_][where])
+                gr(T_LOOP[kk_][where])
+
+            pl.when(i == kk_)(here)
+
+    mg(G_MLP)
     lax.fori_loop(0, 4, mlp_body, 0)
 
     def bwd2_body(i, _):
@@ -557,6 +679,7 @@
     send(ga.at[mine_rows], ga.at[mine_rows], S_GA, R_GA, dev_pair, lambda: ga.at[mine_rows])
     when(swap, lambda: send(bo, bo_out, S_BO, R_BO, dev_swap, lambda: bo, swap))
     w_bo = local(lambda: bo, lambda: bo_out, keep)
+    gr(T_BWD2)
     wrecv(ga.at[pair_rows], R_GA)
 
     def dctx_body(i, _):
@@ -569,110 +692,42 @@
         return 0
 
     lax.fori_loop(0, NB, dctx_body, 0)
-
-    def a_s1(hp):
-        g = gatt.at[hp]
-        send(g.at[r_op, pl.ds(0, 64)], a1b.at[hp, 0], S_A1 + 2 * hp, R_A1 + 2 * hp, dev_up, lambda: a1b.at[hp, 0])
-        send(g.at[r_op, pl.ds(64, 64)], a1b.at[hp, 1], S_A1 + 2 * hp + 1, R_A1 + 2 * hp + 1, dev_dn,
-             lambda: a1b.at[hp, 1])
-
-    def a_s2(hp):
-        g = gatt.at[hp]
-        wrecv(a1b.at[hp, 0], R_A1 + 2 * hp)
-        add_into(g.at[r_up, pl.ds(0, 64)], a1b.at[hp, 0])
-        send(g.at[r_up], a2b.at[hp, 0], S_A2 + 2 * hp, R_A2 + 2 * hp, dev_up, lambda: a2b.at[hp, 0])
-        wrecv(a1b.at[hp, 1], R_A1 + 2 * hp + 1)
-        add_into(g.at[r_dn, pl.ds(64, 64)], a1b.at[hp, 1])
-        send(g.at[r_dn], a2b.at[hp, 1], S_A2 + 2 * hp + 1, R_A2 + 2 * hp + 1, dev_dn, lambda: a2b.at[hp, 1])
-
-    parts = [(0, 0, 128, 0, 0), (1, 0, 64, 0, 128), (1, 64, 64, 1, 0), (2, 0, 128, 1, 64)]
-
-    def a_s3(hp):
-        g = gatt.at[hp]
-        wrecv(a2b.at[hp, 0], R_A2 + 2 * hp)
-        wrecv(a2b.at[hp, 1], R_A2 + 2 * hp + 1)
-        add_into(g.at[r], a2b.at[hp, 0], a2b.at[hp, 1])
-        for pi, (ph, lo, n, zz, to) in enumerate(parts):
-            if ph != hp:
-                continue
-
-            def go(pi=pi, lo=lo, n=n, zz=zz, to=to):
-                zd = 2 * c + zz
-                slot = (zd - z + 3) % 4
-                send(g.at[r, pl.ds(lo, n)], azb.at[slot, pl.ds(to, n)], S_AZ + pi,
-                     R_AZ + 3 * pi + slot, (dp, zd), lambda: gatt.at[hp, 0, pl.ds(lo, n)], need(zz))
-
-            pl.when(need(zz))(go)
-
-    def a_fin(zz):
-        for pi, (ph, lo, n, zo, to) in enumerate(parts):
-            if zo != zz:
-                continue
-            for slot in range(3):
-                wrecv(azb.at[slot, pl.ds(to, n)], R_AZ + 3 * pi + slot)
-            t = gatt[ph, r, lo : lo + n].astype(F32)
-            for slot in range(3):
-                t = t + azb[slot, to : to + n].astype(F32)
-            fa[to : to + n] = t.astype(BF)
-
-    def a_ag():
-        for i, dev in enumerate((dev_up, dev_dn, dev_pair)):
-            send(fa, ga_out.at[r], S_HA + i, R_HA + i, dev, lambda: fa, own_c)
-
-    def a_ag2():
-        lo = ga_out.at[r_dn, pl.ds(0, half)]
-        hi = ga_out.at[r_up, pl.ds(half, half)]
-        wrecv(ga_out.at[r_dn], R_HA)
-        send(lo, lo, S_HB, R_HB, dev_up, lambda: fa.at[pl.ds(0, half)], own_c)
-        send(ga_out.at[r_dn], ga_out.at[r_dn], S_HC, R_HC, dev_pair, lambda: fa, own_c)
-        wrecv(ga_out.at[r_up], R_HA + 1)
-        send(hi, hi, S_HB + 1, R_HB + 1, dev_dn, lambda: fa.at[pl.ds(0, half)], own_c)
-        send(ga_out.at[r_up], ga_out.at[r_up], S_HC + 1, R_HC + 1, dev_pair, lambda: fa, own_c)
-
-    def a_ag3():
-        wrecv(ga_out.at[r_op, pl.ds(0, half)], R_HB)
-        wrecv(ga_out.at[r_op, pl.ds(half, half)], R_HB + 1)
-        send(ga_out.at[r_op], ga_out.at[r_op], S_HC + 2, R_HC + 2, dev_pair, lambda: fa, own_c)
-
-    def a_end():
-        wrecv(ga_out.at[r], R_HA + 2)
-        wrecv(ga_out.at[r_dn], R_HC)
-        wrecv(ga_out.at[r_up], R_HC + 1)
-        wrecv(ga_out.at[r_op], R_HC + 2)
-
-    def bwd_head(hp, hh):
-        h = hp * 2 + hh
-        lanes, inhead = head_prep(hp, hh)
-        hrows = pl.ds(al(h * 64, 64), 64)
-        vh[...] = jnp.where(inhead, v[:, lanes].astype(F32), 0.0).astype(BF)
-        dl = jnp.sum(dot_[hrows, :].astype(F32) * ot[hrows, :].astype(F32), axis=0, keepdims=True)
-        ls_h = lse[h]
+    gr(T_DCTX)
+
+    def bwd_pair(hp, _):
+        prep = []
+        for hh in (0, 1):
+            h = hp * 2 + hh
+            lanes, inhead = head_prep(hp, hh)
+            hrows = pl.ds(al(h * 64, 64), 64)
+            vh[hh] = jnp.where(inhead, v[:, lanes].astype(F32), 0.0).astype(BF)
+            dl = jnp.sum(dot_[hrows, :].astype(F32) * ot[hrows, :].astype(F32), axis=0, keepdims=True)
+            prep.append((h, hrows, dl, lse[h]))
         for kb in range(NB):
             krows = slice(kb * BQ, kb * BQ + BQ)
             qs = slice(kb * BQ, T)
-            s = dot(kh[krows, :], qh[:, qs])
-            diag = s[:, :BQ] + cmask[...]
-            s = diag if kb == NB - 1 else jnp.concatenate([diag, s[:, BQ:]], axis=1)
-            p = jnp.exp2(s * CS - ls_h[0:1, qs])
-            dpr = dot(vh[krows, :], dot_[lanes, qs])
-            ds = (p * (dpr - dl[:, qs])).astype(BF)
-            dv = dot(p.astype(BF), do[qs, lanes])
-            dk = dot(ds, q[qs, lanes]) * 0.125
-            v[krows, lanes] = jnp.where(inhead, dv, v[krows, lanes].astype(F32)).astype(BF)
-            k[krows, lanes] = jnp.where(inhead, dk, k[krows, lanes].astype(F32)).astype(BF)
-            piece = dot(kt[hrows, krows], ds)
-            if kb == 0:
-                dqa[...] = piece
-            else:
-                dqa[:, qs] += piece
-        qt[hrows, :] = (dqa[...] * 0.125).astype(BF)
-
-    def bwd_pair(hp, _):
-        def head(hh, _):
-            bwd_head(hp, hh)
-            return 0
-
-        lax.fori_loop(0, 2, head, 0)
+            dks, dvs = [], []
+            for hh in (0, 1):
+                h, hrows, dl, ls_h = prep[hh]
+                s = dot(kh[hh, krows, :], qh[hh, :, qs])
+                diag = s[:, :BQ] + cmask[...]
+                s = diag if kb == NB - 1 else jnp.concatenate([diag, s[:, BQ:]], axis=1)
+                p = jnp.exp2(s * CS - ls_h[0:1, qs])
+                dpr = dot(vh[hh, krows, :], dot_[lanes, qs])
+                ds = (p * (dpr - dl[:, qs])).astype(BF)
+                dvs.append(dot(p.astype(BF), do[qs, lanes]))
+                dks.append(dot(ds, q[qs, lanes]) * 0.125)
+                piece = dot(kt[hrows, krows], ds)
+                if kb == 0:
+                    dqa[hh] = piece
+                else:
+                    dqa[hh, :, qs] += piece
+            first = lane < 64
+            v[krows, lanes] = jnp.where(first, dvs[0], dvs[1]).astype(BF)
+            k[krows, lanes] = jnp.where(first, dks[0], dks[1]).astype(BF)
+            by_pair(hp, gr, [T_ATT[j][kb] for j in range(3)])
+        for hh in (0, 1):
+            qt[prep[hh][1], :] = (dqa[hh] * 0.125).astype(BF)
         lanes = pl.ds(al(hp * 128, 128), 128)
 
         def tr2(i, _):
@@ -687,33 +742,8 @@
             gatt[hp, t] = dot(ref[lanes, :], n1[...]).astype(BF)
         gatt[hp, 3] = dot(ot[lanes, :], ga[...]).astype(BF)
         for j in range(3):
-            pl.when(hp == j)(functools.partial(after_pair, j))
-        return 0
-
-    def after_pair(j):
-        if j == 0:
-            for i in range(3):
-                for m in (1, 0):
-                    g_s2(m, i)
-            for m in (1, 0):
-                g_s1(m, 3)
-            a_s1(0)
-        if j == 1:
-            for i in range(3):
-                for m in (1, 0):
-                    g_s3(m, i)
-            for m in (1, 0):
-                g_s2(m, 3)
-            a_s2(0)
-            a_s1(1)
-        if j == 2:
-            for m in (1, 0):
-                g_s3(m, 3)
-            a_s2(1)
-            a_s1(2)
-            a_s3(0)
-            for m in (1, 0):
-                g_fin(m)
+            pl.when(hp == j)(functools.partial(gr, T_PAIR[j]))
+        return 0
 
     lax.fori_loop(0, 3, bwd_pair, 0)
 
@@ -722,12 +752,11 @@
 
     ps2[...] = dx(pair_rows).astype(BF)
     send(ps2, pr2, S_DX, R_DX, dev_pair, lambda: ps2)
-    a_s2(2)
-    a_s3(1)
-    for m in (1, 0):
-        g_ag(m)
+    gr(T_DX)
+    g_fin(1)
+    g_fin(0)
     dn2[...] = dx(mine_rows)
-    a_s3(2)
+    gr(T_DX2)
     sb[pl.ds(10 + c, 1), :] = jnp.concatenate(
         [jnp.sum(q[...].astype(F32), axis=0, keepdims=True), jnp.sum(v[...].astype(F32), axis=0, keepdims=True)],
         axis=1,
@@ -744,44 +773,66 @@
         gi[rows, :] = (mid[rows, :] + (e - em - n * en) * rstd).astype(BF)
         sb[0:1, :] += jnp.sum(dn * n, axis=0, keepdims=True)
         sb[1:2, :] += jnp.sum(dn, axis=0, keepdims=True)
-        return 0
-
+        for j in range(R // LB):
+            def out(j=j):
+                part = pl.ds(j * LB, LB)
+                send(gi.at[part], gi_out.at[part], S_GI + j, R_GI + j, dev_swap, lambda: gi.at[part], swap)
+
+            pl.when((i == j) & swap)(out)
+        return 0
+
+    g_ag(1)
+    g_ag(0)
     lax.fori_loop(0, R // LB, bwd1_body, 0)
-    when(swap, lambda: send(gi, gi_out, S_GI, R_GI, dev_swap, lambda: gi, swap))
+    gr(T_LAST)
     w_gi = local(lambda: gi, lambda: gi_out, keep)
 
-    p_ra = (ring_dp(r + 1 - 2 * (r % 2), c), z)
-    p_rb = (ring_dp((r + 3 + 2 * (r % 2)) % RING, c), z)
-    stages = [dev_pair, p_ra, p_rb, (dp, z_x), dev_z[2]]
-
-    def small_step(j):
-        send(sb.at[pl.ds(16 * j, 16)], srb.at[j], S_SM + j, R_SM + j, stages[j], lambda: srb.at[j])
-
-    def small_add(j):
-        wrecv(srb.at[j], R_SM + j)
-        t = sb[16 * j : 16 * j + 16] + srb[j]
-        if j < 4:
-            sb[16 * j + 16 : 16 * j + 32] = t
-        else:
-            small_out[...] = t
-
-    small_step(0)
+    def small_pair():
+        send(sb.at[pl.ds(0, 16)], srb.at[8], S_SM, R_SM + 8, dev_pair, lambda: srb.at[0])
+
+    def small_ring():
+        wrecv(srb.at[8], R_SM + 8)
+        t = sb[0:16] + srb[8]
+        sb[16:32] = t
+        srb[r] = t
+        for j, dev in enumerate((dev_up, dev_dn, dev_op)):
+            send(sb.at[pl.ds(16, 16)], srb.at[r], S_SM + 1 + j, R_SM + r, dev, lambda: srb.at[0])
+
+    def small_z():
+        for o in (r_up, r_dn, r_op):
+            wrecv(srb.at[o], R_SM + o)
+        t = (srb[0] + srb[1]) + (srb[2] + srb[3])
+        sb[32:48] = t
+        srb[4 + z] = t
+        for dz in (1, 2, 3):
+            send(sb.at[pl.ds(32, 16)], srb.at[4 + z], S_SM + 3 + dz, R_SM + 4 + z, dev_z[dz], lambda: srb.at[0])
+
+    def small_end():
+        for dz in (1, 2, 3):
+            wrecv(srb.at[4 + zsh(dz)], R_SM + 4 + zsh(dz))
+        t = (srb[4] + srb[5]) + (srb[6] + srb[7])
+        sb[48:64] = t
+        small_out[0:6, :] = t[0:6]
+        small_out[6:7, :] = sb[pl.ds(54 + z, 1), :]
+        row = sb[pl.ds(58 + z // 2, 1), :]
+        odd = (z % 2).astype(F32)
+        even = 1.0 - odd
+        bq = even * row[:, :ZS] + odd * row[:, ZS : 2 * ZS]
+        bv = even * row[:, 2 * ZS : 3 * ZS] + odd * row[:, 3 * ZS :]
+        gap = jnp.zeros((1, HC - ZS), F32)
+        small_out[7:8, :] = jnp.concatenate([bq, gap, bv, gap], axis=1)
+
+    small_pair()
     for m in (1, 0):
         g_ag2(m)
-    small_add(0)
-    small_step(1)
+    small_ring()
     for zz in (0, 1):
         when(z == 2 * c + zz, functools.partial(a_fin, zz))
     when(own_c, a_ag)
-    small_add(1)
-    small_step(2)
+    small_z()
     when(own_c, a_ag2)
-    small_add(2)
-    small_step(3)
     when(own_c, a_ag3)
-    small_add(3)
-    small_step(4)
-    small_add(4)
+    small_end()
 
     w_fs = [local(lambda: fs.at[0], lambda: gm_out.at[0, r, c]), local(lambda: fs.at[1], lambda: gm_out.at[1, r, c])]
     w_fa = local(lambda: fa, lambda: ga_out.at[r], own_c)
@@ -794,9 +845,39 @@
         g_end(m)
     when(not_own, a_end)
     when(swap, lambda: wrecv(bo_out, R_BO))
-    when(swap, lambda: wrecv(gi_out, R_GI))
+    for j in range(R // LB):
+        when(swap, lambda: wrecv(gi_out.at[pl.ds(j * LB, LB)], R_GI + j))
     for sid, (ref, cond) in pending.items():
         when(cond, lambda sid=sid, ref=ref: wsend(ref(), sid))
+
+
+def widen_kernel(bo, gi, gm, ga, bo_o, gi_o, fc_o, proj_o, qkv_o, out_o):
+    bo_o[...] = bo[...]
+    gi_o[...] = gi[...]
+    fc_o[...] = gm[0].astype(F32)
+    proj_o[...] = gm[1].astype(F32)
+    qkv_o[...] = ga[:3].astype(F32)
+    out_o[...] = ga[3].astype(F32)
+
+
+def widen(bo, gi, gm, ga):
+    n = 4
+    (R, D), ZS = bo.shape, ga.shape[1]
+    rows = lambda m: pl.BlockSpec((m // n, D), lambda i: (i, 0))
+    stack = lambda k, m: pl.BlockSpec((k, m // n, D), lambda i: (0, i, 0))
+    return pl.pallas_call(
+        widen_kernel,
+        grid=(n,),
+        out_shape=(
+            jax.ShapeDtypeStruct((R, D), BF), jax.ShapeDtypeStruct((R, D), BF),
+            jax.ShapeDtypeStruct((D, D), F32), jax.ShapeDtypeStruct((D, D), F32),
+            jax.ShapeDtypeStruct((3, ZS, D), F32), jax.ShapeDtypeStruct((ZS, D), F32),
+        ),
+        in_specs=[rows(R), rows(R), stack(2, D), stack(4, ZS)],
+        out_specs=(rows(R), rows(R), rows(D), rows(D), stack(3, ZS), rows(ZS)),
+        compiler_params=pltpu.CompilerParams(vmem_limit_bytes=64 * 1024 * 1024 - 65536),
+        name="widen",
+    )(bo, gi, gm, ga)
 
 
 def body(
@@ -806,33 +887,32 @@
     R, D = hidden_in.shape
     T, HC, ZS, EB = 2 * R, D // 2, D // 4, D // 8
     z = lax.axis_index("tensor")
-    lens = jnp.broadcast_to(jnp.where(z // 2 == 0, lengths[0], lengths[1]).astype(F32), (8, 128))
-    zero = jnp.zeros((ZS,), BF)
     odd = z % 2 == 1
-    qv_row = jnp.concatenate(
-        [
-            jnp.where(odd, zero, b_query), jnp.where(odd, b_query, zero),
-            jnp.where(odd, zero, b_value), jnp.where(odd, b_value, zero),
-        ]
-    )
-    blank = jnp.zeros((D,), BF)
-    bias = jnp.stack([b_fc, qv_row] + [blank] * 6).astype(F32)
-    vecs = jnp.stack([ln1_gain, ln1_bias, b_out, ln2_gain, ln2_bias, b_proj, blank, blank]).astype(F32)
+    lo, hi = (lambda t: jnp.pad(t, (0, HC - ZS))), (lambda t: jnp.pad(t, (HC - ZS, 0)))
+    place = lambda t: jnp.where(odd, hi(t), lo(t))
+    qv_row = jnp.pad(place(b_query), (0, HC)) + jnp.pad(place(b_value), (HC, 0))
+    row = lax.broadcasted_iota(jnp.int32, (16, D), 0)
+    vecs = jnp.zeros((16, D), BF)
+    for at_row, vec in (
+        (0, ln1_gain), (1, ln1_bias), (2, b_out), (3, ln2_gain), (4, ln2_bias), (5, b_proj), (8, b_fc), (9, qv_row),
+    ):
+        vecs = jnp.where(row == at_row, vec[None, :], vecs)
+    vecs = vecs.astype(F32)
     wq = jnp.transpose(w_qkv, (1, 2, 0))
     wf = w_fc.reshape(4, 2, EB, D)
     wp = w_proj.reshape(4, 2, EB, D)
     vm = lambda *s: pltpu.VMEM(s, BF)
     vf = lambda *s: pltpu.VMEM(s, F32)
     scratch = [
-        vf(8, 128), vf(4, 8, D), vm(R, D), vm(R, D), vm(T, D), vm(4, HC, D), vm(2, 4, 4, 2, EB, D),
+        vf(8, 128), vf(8, 128), vf(4, 8, D), vm(R, D), vm(R, D), vm(T, D), vm(4, HC, D), vm(2, 4, 4, 2, EB, D),
         vm(T, HC), vm(T, HC), vm(T, HC), vm(HC, T), vm(HC, T), vm(HC, T),
         vm(T, HC), vm(HC, T), vm(HC, T), vm(T, HC),
         vf(R, D), vm(R, D), vf(R, D), vf(R, D), vm(R, D), vm(R, D), vm(T, D),
         vm(R, D), vm(R, D), vm(R, D), vm(R, D), vm(R, D), vm(R, D),
-        vf(6, 1, T), vf(64, T), vf(256, 256), vm(T, 128), vm(T, 128), vm(128, T),
+        vf(6, 1, T), vf(2, 64, T), vf(256, 256), vm(2, T, 128), vm(2, T, 128), vm(2, 128, T),
         vm(8, 4, EB, D), vm(8, 2, EB // 2, D), vm(8, 2, EB, D), vm(2, 3, EB, D), vm(2, EB, D),
         vm(3, 4, 128, D), vm(3, 2, 64, D), vm(3, 2, 128, D), vm(3, ZS, D), vm(ZS, D),
-        vf(80, D), vf(5, 16, D),
+        vf(64, D), vf(9, 16, D),
         pltpu.SemaphoreType.DMA((SID.n,)), pltpu.SemaphoreType.DMA((RID.n,)), pltpu.SemaphoreType.DMA((12,)),
     ]
     anyspec = pl.BlockSpec(memory_space=pl.ANY)
@@ -844,32 +924,30 @@
             jax.ShapeDtypeStruct((R, D), BF),
             jax.ShapeDtypeStruct((2, 4, 2, EB, D), BF),
             jax.ShapeDtypeStruct((4, ZS, D), BF),
-            jax.ShapeDtypeStruct((16, D), F32),
+            jax.ShapeDtypeStruct((8, D), F32),
         ),
-        in_specs=[vspec] * 3 + [anyspec] * 6,
+        in_specs=[pl.BlockSpec(memory_space=pltpu.SMEM), vspec] + [anyspec] * 6,
         out_specs=(anyspec, anyspec, anyspec, anyspec, vspec),
         scratch_shapes=scratch,
         compiler_params=pltpu.CompilerParams(
             collective_id=0, has_side_effects=True, vmem_limit_bytes=64 * 1024 * 1024 - 65536
         ),
         name="layer",
-    )(lens, bias, vecs, hidden_in, out_grad, wq, w_out, wf, wp)
+    )(lengths, vecs, hidden_in, out_grad, wq, w_out, wf, wp)
     data_count = lax.axis_size("dp")
-    gm = gm.astype(F32)
-    gatt = gatt.astype(F32)
+    gm = gm.reshape(2, D, D)
     if data_count > GROUP:
         groups = [list(range(s, data_count, GROUP)) for s in range(GROUP)]
-        gm, gatt, small = (lax.psum(t, "dp", axis_index_groups=groups) for t in (gm, gatt, small))
-    g_fc = gm[0].reshape(D, D)
-    g_proj = gm[1].reshape(D, D)
-    g_qkv = jnp.transpose(gatt[:3], (2, 0, 1))
-    b_fc_g = lax.dynamic_index_in_dim(small, 6 + z, 0, keepdims=False)
-    b_row = lax.dynamic_index_in_dim(small, 10 + z // 2, 0, keepdims=False)
-    gbq = jnp.where(odd, b_row[ZS : 2 * ZS], b_row[:ZS])
-    gbv = jnp.where(odd, b_row[3 * ZS :], b_row[2 * ZS : 3 * ZS])
+        gm, gatt, small = (
+            lax.psum(t.astype(F32), "dp", axis_index_groups=groups) for t in (gm, gatt, small)
+        )
+    block_out, grad_input, g_fc, g_proj, g_qkv, g_out = widen(block_out, grad_input, gm, gatt)
+    g_qkv = jnp.transpose(g_qkv, (2, 0, 1))
+    gbq = small[7, :ZS]
+    gbv = small[7, HC : HC + ZS]
     return (
-        block_out, grad_input, small[0], small[1], g_qkv, gbq, gbv, gatt[3], small[4],
-        small[2], small[3], g_fc, b_fc_g, g_proj, small[5],
+        block_out, grad_input, small[0], small[1], g_qkv, gbq, gbv, g_out, small[4],
+        small[2], small[3], g_fc, small[6], g_proj, small[5],
     )
 
 

time: 215 us -> 178 us (0.83)
  the two profiles are of different devices: /device:TPU:1 before, /device:TPU:25 now
where the time goes in v2:
time: 178 us
  Pallas kernels  172 us (97%)
  local copies, waits for them, and re-layouts  2.95 us (2%)
  other arithmetic  2.34 us (1%)
    pallas_call x1, Pallas kernels, body(): pl.pallas_call(kernel, out_shape=(jax.ShapeDtypeStruct((R, D), BF), jax.S...  166 us
    pallas_call x1, Pallas kernels, widen(): pl.pallas_call(widen_kernel, grid=(n,), out_shape=(jax.ShapeDtypeStruct((...  6.11 us

profile of v2, /device:TPU:25, one launch (start us, length us, event | category | flops | bytes accessed | tf_op | source)
XLA Modules:
  0.0 178.0 jit_solution(7302402348371097960)
XLA Ops:
  0.7 0.8 pad_select_fusion
  1.5 1.5 select_convert_fusion.vecs
  3.0 165.9 %layer.1 = (bf16[512,768]{1,0:T(8,128)(2,1)}, bf16[512,768]{1,0:T(8,128)(2,1)}, bf16[2,4,2,96,768]{4,3,2,1,0:T(8,128)(2,1)}, bf16[4,192,768]{2,1,0:T(8,128)(2,1)}, f32[8,768]{1,0:T(8,128)}) custom-call(s32[2]{0:T(128)} %lengths.1, f32[16,768]{1,0:T(8,128)} %select_convert_fusion.vecs, bf16[512,768]{1,0:T(8,128)(2,1)} %hid_in.1, bf16[512,768]{1,0:T(8,128)(2,1)} %og_in.1, ...), custom_call_target="tpu_custom_call" | custom-call | tf_op jit(solution)/shard_map/layer/pallas_call | solution.py:920
  169.0 6.1 %widen.1 = (bf16[512,768]{1,0:T(8,128)(2,1)}, bf16[512,768]{1,0:T(8,128)(2,1)}, f32[768,768]{1,0:T(8,128)}, f32[768,768]{1,0:T(8,128)}, f32[3,192,768]{2,1,0:T(8,128)}, /*index=5*/f32[192,768]{1,0:T(8,128)}) custom-call(bf16[512,768]{1,0:T(8,128)(2,1)} %get-tuple-element.26.bo, bf16[512,768]{1,0:T(8,128)(2,1)} %get-tuple-element.27.gi, ...), custom_call_target="tpu_custom_call" | custom-call | tf_op jit(solution)/shard_map/widen/pallas_call | solution.py:868
  175.1 1.7 slice_reduce_fusion
  176.7 1.3 fusion
  (5 shorter events, 0.0 us)

commit v3 on v2

--- a/solution.py
+++ b/solution.py
@@ -20,11 +20,13 @@
 T_LOOP = (("", "10"), ("11 20", "12"), ("13 21", "14"), ("15 22", "16"))
 T_BWD2 = "17 23 30"
 T_DCTX = "31"
-T_ATT = (("24", "32", "25", "33"), ("26", "34", "27", "35"), ("28", "36", "29", "37"))
-T_PAIR = ("18", "19", "110")
-T_DX = "38"
-T_DX2 = "210 39"
-T_LAST = "310"
+T_ATT = (("24", "32", "25", "33"), ("26", "34", "27", "35"), ("28 36", "29", "37 210", "211"))
+T_PAIR = ("18 19", "110 111", "112 113 41 40")
+T_DX = "38 39"
+T_DX2 = "212 213 310 311"
+T_AG = "51 50"
+T_LAST = "312 313"
+T_AG2 = "61 60"
 G_EARLY = ""
 G_QKV = "a0"
 G_TR = ""
@@ -61,31 +63,31 @@
 
 
 SID = Ids()
-S_LEN, S_BIAS, S_HID, S_OG, S_AS1 = SID(1), SID(3), SID(1), SID(1), SID(3)
-S_ARA, S_ARB = SID(4), SID(4)
+S_LEN, S_BIAS, S_HID, S_OG, S_AS1 = SID(1), SID(3), SID(1), SID(1), SID(6)
+S_ARA, S_ARB = SID(8), SID(8)
 S_MS1, S_MRA, S_MRB, S_MP = SID(6), SID(12), SID(12), SID(6)
 S_N1, S_PO, S_GA, S_DX, S_BO, S_GI = SID(1), SID(1), SID(1), SID(1), SID(1), SID(8)
 S_GP, S_G1, S_G2, S_GZ = SID(8), SID(16), SID(16), SID(8)
 S_FA, S_FB, S_FC = SID(6), SID(4), SID(6)
-S_A1, S_A2, S_AZ = SID(6), SID(6), SID(4)
-S_HA, S_HB, S_HC = SID(3), SID(2), SID(3)
+S_A1, S_A2, S_AZ = SID(12), SID(12), SID(6)
+S_HA, S_HB, S_HC = SID(9), SID(6), SID(9)
 S_SM = SID(7)
 RID = Ids()
-R_LEN, R_BIAS, R_HID, R_OG, R_AS1 = RID(1), RID(3), RID(1), RID(1), RID(2)
-R_ARA, R_ARB = RID(4), RID(4)
+R_LEN, R_BIAS, R_HID, R_OG, R_AS1 = RID(1), RID(3), RID(1), RID(1), RID(4)
+R_ARA, R_ARB = RID(8), RID(8)
 R_MS1, R_MRA, R_MRB, R_MP = RID(6), RID(12), RID(12), RID(6)
 R_N1, R_PO, R_GA, R_DX, R_BO, R_GI = RID(1), RID(1), RID(1), RID(1), RID(1), RID(8)
 R_GP, R_G1, R_G2, R_GZ = RID(8), RID(16), RID(16), RID(6)
 R_FA, R_FB, R_FC = RID(6), RID(4), RID(6)
-R_A1, R_A2, R_AZ = RID(6), RID(6), RID(12)
-R_HA, R_HB, R_HC = RID(3), RID(2), RID(3)
+R_A1, R_A2, R_AZ = RID(12), RID(12), RID(18)
+R_HA, R_HB, R_HC = RID(9), RID(6), RID(9)
 R_SM = RID(9)
 
 
 def kernel(
     lengths, vecs, hid_in, og_in, wq, wo, wf, wp,
     bo_out, gi_out, gm_out, ga_out, small_out,
-    lens, lrecv, bfa, hid, og, n1, watt, wmlp, q, k, v, qt, kt, vt, do, dot_, ot, ctx,
+    lens, lrecv, bfa, hid, og, n1, watt, wmlp, q, k, v, qt, kt, vt, do, dot_, ot,
     mid, n2, oacc, dn2, act, dpre, ga, ps, pr, ps2, pr2, bo, gi,
     lse, dqa, cmask, kh, vh, qh,
     prb, r1b, r2b, zb, fs, gatt, a1b, a2b, azb, fa, sb, srb,
@@ -125,6 +127,7 @@
     keep = c == z % 2
     swap = c != z % 2
     own_c = z // 2 == c
+    mine = (z == 2 * c, z == 2 * c + 1)
     not_own = z // 2 != c
     zz_own = z % 2
     pending = {}
@@ -173,21 +176,24 @@
     def att_rows(zz):
         return pl.ds(al(zz * ZS, 16), ZS)
 
-    def att_s1():
+    ZQ = ZS // RING
+
+    def att_piece(e, zz, rr):
+        rows = pl.ds(al(zz * ZS + rr * ZQ, 16), ZQ)
+        return watt.at[3, rows] if e else watt.at[pl.ds(0, 3), rows]
+
+    def att_half(e, zz, rr, side):
+        rows = pl.ds(al(zz * ZS + rr * ZQ, 16), ZQ)
+        cols = pl.ds(side * HC, HC)
+        return watt.at[3, rows, cols] if e else watt.at[pl.ds(0, 3), rows, cols]
+
+    def att_s1(e):
         for dz in (1, 2, 3):
-            dst = watt.at[r, att_rows(zz_own)]
-
+            rows = pl.ds(al(r * ZQ, 16), ZQ)
+            src = wo.at[rows] if e else wq.at[:, rows]
             dev = (dp - c + z // 2, (z + dz) % 4)
-
-            def from_q():
-                send(wq.at[jnp.minimum(r, 2)], dst, S_AS1 + dz - 1, R_AS1 + zz_own, dev)
-
-            def from_o():
-                send(wo, dst, S_AS1 + dz - 1, R_AS1 + zz_own, dev)
-
-            pl.when(r < 3)(from_q)
-            pl.when(r == 3)(from_o)
-            pending[S_AS1 + dz - 1] = (lambda: wo, swap)
+            send(src, att_piece(e, zz_own, r), S_AS1 + 3 * e + dz - 1, R_AS1 + 2 * e + zz_own, dev,
+                 lambda: att_piece(e, 0, 0), swap)
 
     w_wq = local(lambda: wq, lambda: watt.at[pl.ds(0, 3), att_rows(zz_own)], own_c)
     w_wo = local(lambda: wo, lambda: watt.at[3, att_rows(zz_own)], own_c)
@@ -282,8 +288,9 @@
     qq = lax.broadcasted_iota(jnp.int32, (BQ, BQ), 1)
     cmask[...] = jnp.where(kk <= qq, 0.0, NEG)
     pl.semaphore_wait(barrier, 10)
-    pl.when(swap)(att_s1)
+    pl.when(swap)(lambda: att_s1(0))
     when(swap, lambda: send(hid_in, hid, S_HID, R_HID, dev_swap, lambda: hid_in, swap))
+    pl.when(swap)(lambda: att_s1(1))
     for dz in (1, 2, 3):
         send(bias, bfa.at[z], S_BIAS + dz - 1, R_BIAS + dz - 1, dev_z[dz], lambda: bias)
     lens[...] = jnp.full((8, 128), lengths[z // 2].astype(F32))
@@ -295,38 +302,41 @@
     def need(zz):
         return needs[zz]
 
-    def ar_a(zz):
-        piece = watt.at[r, att_rows(zz)]
-        wrecv(piece, R_AS1 + zz)
-        send(piece, piece, S_ARA + 2 * zz, R_ARA + 2 * zz, dev_up, lambda: wo, need(zz))
-        send(piece, piece, S_ARA + 2 * zz + 1, R_ARA + 2 * zz + 1, dev_dn, lambda: wo, need(zz))
-
-    def ar_b(zz):
-        wrecv(watt.at[r_dn, att_rows(zz)], R_ARA + 2 * zz)
-        lo = watt.at[r_dn, pl.ds(al(zz * ZS, 16), half)]
-        send(lo, lo, S_ARB + 2 * zz, R_ARB + 2 * zz, dev_up, lambda: watt.at[0, pl.ds(0, half)], need(zz))
-        wrecv(watt.at[r_up, att_rows(zz)], R_ARA + 2 * zz + 1)
-        hi = watt.at[r_up, pl.ds(al(zz * ZS + half, 16), half)]
-        send(hi, hi, S_ARB + 2 * zz + 1, R_ARB + 2 * zz + 1, dev_dn, lambda: watt.at[0, pl.ds(0, half)], need(zz))
-
-    def ar_c(zz):
-        wrecv(watt.at[r_op, pl.ds(al(zz * ZS, 16), half)], R_ARB + 2 * zz)
-        wrecv(watt.at[r_op, pl.ds(al(zz * ZS + half, 16), half)], R_ARB + 2 * zz + 1)
-
-    for zz in (0, 1):
-        when(need(zz), functools.partial(ar_a, zz))
+    def ar_a(e, zz):
+        u = 2 * e + zz
+        piece = att_piece(e, zz, r)
+        wrecv(piece, R_AS1 + u)
+        for j, dev in enumerate((dev_up, dev_dn)):
+            send(piece, piece, S_ARA + 2 * u + j, R_ARA + 2 * u + j, dev, lambda: att_piece(e, 0, 0), need(zz))
+
+    def ar_b(e, zz):
+        u = 2 * e + zz
+        for j, (dev, rr) in enumerate(((dev_up, r_dn), (dev_dn, r_up))):
+            wrecv(att_piece(e, zz, rr), R_ARA + 2 * u + j)
+            part = att_half(e, zz, rr, j)
+            send(part, part, S_ARB + 2 * u + j, R_ARB + 2 * u + j, dev, lambda: att_half(e, 0, 0, 0), need(zz))
+
+    def ar_c(e, zz):
+        u = 2 * e + zz
+        for j in (0, 1):
+            wrecv(att_half(e, zz, r_op, j), R_ARB + 2 * u + j)
+
+    def ar(step, e):
+        for zz in (0, 1):
+            when(need(zz), functools.partial(step, e, zz))
+
+    ar(ar_a, 0)
     for dz in (1, 3):
         mg_s1(0, dz)
         mg_s1(1, dz)
-    for zz in (0, 1):
-        when(need(zz), functools.partial(ar_b, zz))
+    ar(ar_b, 0)
     pl.when(swap)(norm_one_far)
+    ar(ar_a, 1)
     mg_s1(0, 2)
     mg_s1(1, 2)
     when(swap, lambda: send(og_in, og, S_OG, R_OG, dev_swap, lambda: og_in, swap))
     mg(G_EARLY)
-    for zz in (0, 1):
-        when(need(zz), functools.partial(ar_c, zz))
+    ar(ar_c, 0)
     w_wq()
     w_wo()
     for dz in (1, 2, 3):
@@ -347,6 +357,7 @@
         return 0
 
     lax.fori_loop(0, NB, qkv_body, 0)
+    ar(ar_b, 1)
     mg(G_QKV)
 
     def tr_body(i, _):
@@ -405,19 +416,12 @@
 
     lax.fori_loop(0, 3, fwd_pair, 0)
 
-    def ctx_body(i, _):
-        rows = pl.ds(al(i * BQ, BQ), BQ)
-        for hp in range(3):
-            lanes = slice(hp * 128, hp * 128 + 128)
-            ctx[rows, lanes] = ot[lanes, rows].T
-        return 0
-
-    lax.fori_loop(0, NB, ctx_body, 0)
+    ar(ar_c, 1)
     mg(G_CTX)
 
-    ps[...] = dot(ctx[pair_rows, :], watt[3]).astype(BF)
+    ps[...] = tn(ot[:, pl.ds(al(oc * R, R), R)], watt[3]).astype(BF)
     send(ps, pr, S_PO, R_PO, dev_pair, lambda: ps)
-    mid[...] = hid[...].astype(F32) + vecs[2:3, :] + dot(ctx[mine_rows, :], watt[3])
+    mid[...] = hid[...].astype(F32) + vecs[2:3, :] + tn(ot[:, pl.ds(al(row0, R), R)], watt[3])
     w_og()
     when(swap, lambda: wrecv(og, R_OG))
     wrecv(pr, R_PO)
@@ -524,82 +528,87 @@
         wrecv(gm_out.at[m, r_up, oc], R_FC + 3 * m + 1)
         wrecv(gm_out.at[m, r_op, oc], R_FC + 3 * m + 2)
 
-    def a_s1(hp):
-        g = gatt.at[hp]
-        send(g.at[r_op, pl.ds(0, 64)], a1b.at[hp, 0], S_A1 + 2 * hp, R_A1 + 2 * hp, dev_up, lambda: a1b.at[hp, 0])
-        send(g.at[r_op, pl.ds(64, 64)], a1b.at[hp, 1], S_A1 + 2 * hp + 1, R_A1 + 2 * hp + 1, dev_dn,
-             lambda: a1b.at[hp, 1])
-
-    def a_s2(hp):
-        g = gatt.at[hp]
-        wrecv(a1b.at[hp, 0], R_A1 + 2 * hp)
-        add_into(g.at[r_up, pl.ds(0, 64)], a1b.at[hp, 0])
-        send(g.at[r_up], a2b.at[hp, 0], S_A2 + 2 * hp, R_A2 + 2 * hp, dev_up, lambda: a2b.at[hp, 0])
-        wrecv(a1b.at[hp, 1], R_A1 + 2 * hp + 1)
-        add_into(g.at[r_dn, pl.ds(64, 64)], a1b.at[hp, 1])
-        send(g.at[r_dn], a2b.at[hp, 1], S_A2 + 2 * hp + 1, R_A2 + 2 * hp + 1, dev_dn, lambda: a2b.at[hp, 1])
-
-    parts = [(0, 0, 128, 0, 0), (1, 0, 64, 0, 128), (1, 64, 64, 1, 0), (2, 0, 128, 1, 64)]
-
-    def a_s3(hp):
-        g = gatt.at[hp]
-        wrecv(a2b.at[hp, 0], R_A2 + 2 * hp)
-        wrecv(a2b.at[hp, 1], R_A2 + 2 * hp + 1)
-        add_into(g.at[r], a2b.at[hp, 0], a2b.at[hp, 1])
-        for pi, (ph, lo, n, zz, to) in enumerate(parts):
-            if ph != hp:
-                continue
-
-            def go(pi=pi, lo=lo, n=n, zz=zz, to=to):
-                zd = 2 * c + zz
-                slot = (zd - z + 3) % 4
-                send(g.at[r, pl.ds(lo, n)], azb.at[slot, pl.ds(to, n)], S_AZ + pi,
-                     R_AZ + 3 * pi + slot, (dp, zd), lambda: gatt.at[hp, 0, pl.ds(lo, n)], need(zz))
-
-            pl.when(need(zz))(go)
-
-    def a_fin(zz):
-        for pi, (ph, lo, n, zo, to) in enumerate(parts):
-            if zo != zz:
-                continue
+    def hat(h):
+        return gatt.at[h // 2], (h % 2) * 64
+
+    def a_s1(h):
+        g, o = hat(h)
+        for j, dev in enumerate((dev_up, dev_dn)):
+            send(g.at[r_op, pl.ds(o + 32 * j, 32)], a1b.at[h, j], S_A1 + 2 * h + j, R_A1 + 2 * h + j, dev,
+                 lambda j=j: a1b.at[h, j])
+
+    def a_s2(h):
+        g, o = hat(h)
+        for j, (dev, rr) in enumerate(((dev_up, r_up), (dev_dn, r_dn))):
+            wrecv(a1b.at[h, j], R_A1 + 2 * h + j)
+            add_into(g.at[rr, pl.ds(o + 32 * j, 32)], a1b.at[h, j])
+            send(g.at[rr, pl.ds(o, 64)], a2b.at[h, j], S_A2 + 2 * h + j, R_A2 + 2 * h + j, dev,
+                 lambda j=j: a2b.at[h, j])
+
+    def a_s3(h):
+        g, o = hat(h)
+        for j in (0, 1):
+            wrecv(a2b.at[h, j], R_A2 + 2 * h + j)
+        add_into(g.at[r, pl.ds(o, 64)], a2b.at[h, 0], a2b.at[h, 1])
+        zz, to = h // 3, (h % 3) * 64
+
+        def go():
+            zd = 2 * c + zz
+            slot = (zd - z + 3) % 4
+            send(g.at[r, pl.ds(o, 64)], azb.at[slot, pl.ds(to, 64)], S_AZ + h, R_AZ + 3 * h + slot, (dp, zd),
+                 lambda: a2b.at[h, 0], need(zz))
+
+        pl.when(need(zz))(go)
+
+    def a_fin(jj):
+        def go(zz):
+            h = 3 * zz + jj
+            g, o = hat(h)
             for slot in range(3):
-                wrecv(azb.at[slot, pl.ds(to, n)], R_AZ + 3 * pi + slot)
-            t = gatt[ph, r, lo : lo + n].astype(F32)
+                wrecv(azb.at[slot, pl.ds(jj * 64, 64)], R_AZ + 3 * h + slot)
+            t = g[r, o : o + 64].astype(F32)
             for slot in range(3):
-                t = t + azb[slot, to : to + n].astype(F32)
-            fa[to : to + n] = t.astype(BF)
-
-    def a_ag():
+                t = t + azb[slot, jj * 64 : jj * 64 + 64].astype(F32)
+            fa[jj * 64 : jj * 64 + 64] = t.astype(BF)
+
+        for zz in (0, 1):
+            when(mine[zz], functools.partial(go, zz))
+
+    def a_ag(jj):
+        part = fa.at[pl.ds(jj * 64, 64)]
         for i, dev in enumerate((dev_up, dev_dn, dev_pair)):
-            send(fa, ga_out.at[r], S_HA + i, R_HA + i, dev, lambda: fa, own_c)
-
-    def a_ag2():
-        lo = ga_out.at[r_dn, pl.ds(0, half)]
-        hi = ga_out.at[r_up, pl.ds(half, half)]
-        wrecv(ga_out.at[r_dn], R_HA)
-        send(lo, lo, S_HB, R_HB, dev_up, lambda: fa.at[pl.ds(0, half)], own_c)
-        send(ga_out.at[r_dn], ga_out.at[r_dn], S_HC, R_HC, dev_pair, lambda: fa, own_c)
-        wrecv(ga_out.at[r_up], R_HA + 1)
-        send(hi, hi, S_HB + 1, R_HB + 1, dev_dn, lambda: fa.at[pl.ds(0, half)], own_c)
-        send(ga_out.at[r_up], ga_out.at[r_up], S_HC + 1, R_HC + 1, dev_pair, lambda: fa, own_c)
-
-    def a_ag3():
-        wrecv(ga_out.at[r_op, pl.ds(0, half)], R_HB)
-        wrecv(ga_out.at[r_op, pl.ds(half, half)], R_HB + 1)
-        send(ga_out.at[r_op], ga_out.at[r_op], S_HC + 2, R_HC + 2, dev_pair, lambda: fa, own_c)
+            send(part, ga_out.at[r, pl.ds(jj * 64, 64)], S_HA + 3 * jj + i, R_HA + 3 * jj + i, dev,
+                 lambda: fa.at[pl.ds(0, 64)], own_c)
+
+    def a_ag2(jj):
+        for j, (dev, rr) in enumerate(((dev_up, r_dn), (dev_dn, r_up))):
+            part = ga_out.at[rr, pl.ds(jj * 64, 64)]
+            wrecv(part, R_HA + 3 * jj + j)
+            piece = ga_out.at[rr, pl.ds(jj * 64 + 32 * j, 32)]
+            send(piece, piece, S_HB + 2 * jj + j, R_HB + 2 * jj + j, dev, lambda: fa.at[pl.ds(0, 32)], own_c)
+            send(part, part, S_HC + 3 * jj + j, R_HC + 3 * jj + j, dev_pair, lambda: fa.at[pl.ds(0, 64)], own_c)
+
+    def a_ag3(jj):
+        for j in (0, 1):
+            wrecv(ga_out.at[r_op, pl.ds(jj * 64 + 32 * j, 32)], R_HB + 2 * jj + j)
+        part = ga_out.at[r_op, pl.ds(jj * 64, 64)]
+        send(part, part, S_HC + 3 * jj + 2, R_HC + 3 * jj + 2, dev_pair, lambda: fa.at[pl.ds(0, 64)], own_c)
 
     def a_end():
-        wrecv(ga_out.at[r], R_HA + 2)
-        wrecv(ga_out.at[r_dn], R_HC)
-        wrecv(ga_out.at[r_up], R_HC + 1)
-        wrecv(ga_out.at[r_op], R_HC + 2)
+        for jj in range(3):
+            part = pl.ds(jj * 64, 64)
+            wrecv(ga_out.at[r, part], R_HA + 3 * jj + 2)
+            for j, rr in enumerate((r_dn, r_up, r_op)):
+                wrecv(ga_out.at[rr, part], R_HC + 3 * jj + j)
 
     GA_ = 0.7978845608028654
 
     def gr(steps):
         for st in steps.split():
             kind, u = int(st[0]), int(st[1:])
-            if u < 8:
+            if kind > 3:
+                (g_fin, g_ag, g_ag2)[kind - 4](u)
+            elif u < 8:
                 (g_s1, g_s2, g_s3)[kind - 1](1 - u % 2, u // 2)
             else:
                 (a_s1, a_s2, a_s3)[kind - 1](u - 8)
@@ -618,10 +627,10 @@
             fcb = wmlp[0, zp, :, :, :, cols].reshape(D, 256)
             pre = dot(n2[...], fcb) + bfa[zp, 0:1, cols]
             sq = pre * pre
-            t = jnp.tanh(GA_ * (pre + 0.044715 * (pre * sq)))
+            t = jnp.tanh(pre * (GA_ + (0.044715 * GA_) * sq))
             hf = 0.5 * (1.0 + t)
             act[:, cols] = (pre * hf).astype(BF)
-            gp = hf + (0.5 * GA_) * pre * (1.0 - t * t) * (1.0 + 0.134145 * sq)
+            gp = hf * (1.0 + (1.0 - hf) * (pre * (2.0 * GA_ + (0.26829 * GA_) * sq)))
             prj = wmlp[1, zp].reshape(D, D)[cols, :]
             dp_ = (nt(og[...], prj) * gp).astype(BF)
             dpre[:, cols] = dp_
@@ -753,8 +762,6 @@
     ps2[...] = dx(pair_rows).astype(BF)
     send(ps2, pr2, S_DX, R_DX, dev_pair, lambda: ps2)
     gr(T_DX)
-    g_fin(1)
-    g_fin(0)
     dn2[...] = dx(mine_rows)
     gr(T_DX2)
     sb[pl.ds(10 + c, 1), :] = jnp.concatenate(
@@ -781,8 +788,7 @@
             pl.when((i == j) & swap)(out)
         return 0
 
-    g_ag(1)
-    g_ag(0)
+    gr(T_AG)
     lax.fori_loop(0, R // LB, bwd1_body, 0)
     gr(T_LAST)
     w_gi = local(lambda: gi, lambda: gi_out, keep)
@@ -823,15 +829,16 @@
         small_out[7:8, :] = jnp.concatenate([bq, gap, bv, gap], axis=1)
 
     small_pair()
-    for m in (1, 0):
-        g_ag2(m)
+    gr(T_AG2)
     small_ring()
-    for zz in (0, 1):
-        when(z == 2 * c + zz, functools.partial(a_fin, zz))
-    when(own_c, a_ag)
+    for jj in range(3):
+        a_fin(jj)
+        when(own_c, functools.partial(a_ag, jj))
     small_z()
-    when(own_c, a_ag2)
-    when(own_c, a_ag3)
+    for jj in range(3):
+        when(own_c, functools.partial(a_ag2, jj))
+    for jj in range(3):
+        when(own_c, functools.partial(a_ag3, jj))
     small_end()
 
     w_fs = [local(lambda: fs.at[0], lambda: gm_out.at[0, r, c]), local(lambda: fs.at[1], lambda: gm_out.at[1, r, c])]
@@ -906,12 +913,12 @@
     scratch = [
         vf(8, 128), vf(8, 128), vf(4, 8, D), vm(R, D), vm(R, D), vm(T, D), vm(4, HC, D), vm(2, 4, 4, 2, EB, D),
         vm(T, HC), vm(T, HC), vm(T, HC), vm(HC, T), vm(HC, T), vm(HC, T),
-        vm(T, HC), vm(HC, T), vm(HC, T), vm(T, HC),
+        vm(T, HC), vm(HC, T), vm(HC, T),
         vf(R, D), vm(R, D), vf(R, D), vf(R, D), vm(R, D), vm(R, D), vm(T, D),
         vm(R, D), vm(R, D), vm(R, D), vm(R, D), vm(R, D), vm(R, D),
         vf(6, 1, T), vf(2, 64, T), vf(256, 256), vm(2, T, 128), vm(2, T, 128), vm(2, 128, T),
         vm(8, 4, EB, D), vm(8, 2, EB // 2, D), vm(8, 2, EB, D), vm(2, 3, EB, D), vm(2, EB, D),
-        vm(3, 4, 128, D), vm(3, 2, 64, D), vm(3, 2, 128, D), vm(3, ZS, D), vm(ZS, D),
+        vm(3, 4, 128, D), vm(6, 2, 32, D), vm(6, 2, 64, D), vm(3, ZS, D), vm(ZS, D),
         vf(64, D), vf(9, 16, D),
         pltpu.SemaphoreType.DMA((SID.n,)), pltpu.SemaphoreType.DMA((RID.n,)), pltpu.SemaphoreType.DMA((12,)),
     ]

time: 178 us -> 173 us (0.972)
  the two profiles are of different devices: /device:TPU:25 before, /device:TPU:1 now
where the time goes in v3:
time: 173 us; the launch traced here: 172 us
  Pallas kernels  166 us (96%)
  local copies, waits for them, and re-layouts  2.95 us (2%)
  other arithmetic  2.34 us (1%)
    pallas_call x1, Pallas kernels, body(): pl.pallas_call(kernel, out_shape=(jax.ShapeDtypeStruct((R, D), BF), jax.S...  160 us
    pallas_call x1, Pallas kernels, widen(): pl.pallas_call(widen_kernel, grid=(n,), out_shape=(jax.ShapeDtypeStruct((...  6.11 us

profile of v3, /device:TPU:1, one launch (start us, length us, event | category | flops | bytes accessed | tf_op | source)
XLA Modules:
  0.0 172.5 jit_solution(8764517888136585482)
XLA Ops:
  0.7 0.8 pad_select_fusion
  1.5 1.5 select_convert_fusion.vecs
  3.0 160.4 %layer.1 = (bf16[512,768]{1,0:T(8,128)(2,1)}, bf16[512,768]{1,0:T(8,128)(2,1)}, bf16[2,4,2,96,768]{4,3,2,1,0:T(8,128)(2,1)}, bf16[4,192,768]{2,1,0:T(8,128)(2,1)}, f32[8,768]{1,0:T(8,128)}) custom-call(s32[2]{0:T(128)} %lengths.1, f32[16,768]{1,0:T(8,128)} %select_convert_fusion.vecs, bf16[512,768]{1,0:T(8,128)(2,1)} %hid_in.1, bf16[512,768]{1,0:T(8,128)(2,1)} %og_in.1, ...), custom_call_target="tpu_custom_call" | custom-call | tf_op jit(solution)/shard_map/layer/pallas_call | solution.py:927
  163.4 6.1 %widen.1 = (bf16[512,768]{1,0:T(8,128)(2,1)}, bf16[512,768]{1,0:T(8,128)(2,1)}, f32[768,768]{1,0:T(8,128)}, f32[768,768]{1,0:T(8,128)}, f32[3,192,768]{2,1,0:T(8,128)}, /*index=5*/f32[192,768]{1,0:T(8,128)}) custom-call(bf16[512,768]{1,0:T(8,128)(2,1)} %get-tuple-element.26.bo, bf16[512,768]{1,0:T(8,128)(2,1)} %get-tuple-element.27.gi, ...), custom_call_target="tpu_custom_call" | custom-call | tf_op jit(solution)/shard_map/widen/pallas_call | solution.py:875
  169.5 1.7 slice_reduce_fusion
  171.2 1.3 fusion
  (5 shorter events, 0.0 us)

commit v4 on v3

--- a/solution.py
+++ b/solution.py
@@ -858,19 +858,28 @@
         when(cond, lambda sid=sid, ref=ref: wsend(ref(), sid))
 
 
-def widen_kernel(bo, gi, gm, ga, bo_o, gi_o, fc_o, proj_o, qkv_o, out_o):
+def widen_kernel(bo, gi, gm, ga, small, bo_o, gi_o, fc_o, proj_o, qkv_o, out_o, *vec_o):
     bo_o[...] = bo[...]
     gi_o[...] = gi[...]
     fc_o[...] = gm[0].astype(F32)
     proj_o[...] = gm[1].astype(F32)
     qkv_o[...] = ga[:3].astype(F32)
     out_o[...] = ga[3].astype(F32)
-
-
-def widen(bo, gi, gm, ga):
+    for j, o in enumerate(vec_o):
+        if j < 7:
+            o[...] = small[j]
+        else:
+            n = o.shape[0]
+            at = (j - 7) * small.shape[1] // 2
+            o[...] = small[7, at : at + n]
+
+
+def widen(bo, gi, gm, ga, small):
     n = 4
     (R, D), ZS = bo.shape, ga.shape[1]
+    lens = (D,) * 7 + (ZS,) * 2
     rows = lambda m: pl.BlockSpec((m // n, D), lambda i: (i, 0))
+    vec = lambda m: pl.BlockSpec((m,), lambda i: (0,))
     stack = lambda k, m: pl.BlockSpec((k, m // n, D), lambda i: (0, i, 0))
     return pl.pallas_call(
         widen_kernel,
@@ -879,12 +888,13 @@
             jax.ShapeDtypeStruct((R, D), BF), jax.ShapeDtypeStruct((R, D), BF),
             jax.ShapeDtypeStruct((D, D), F32), jax.ShapeDtypeStruct((D, D), F32),
             jax.ShapeDtypeStruct((3, ZS, D), F32), jax.ShapeDtypeStruct((ZS, D), F32),
+            *(jax.ShapeDtypeStruct((m,), F32) for m in lens),
         ),
-        in_specs=[rows(R), rows(R), stack(2, D), stack(4, ZS)],
-        out_specs=(rows(R), rows(R), rows(D), rows(D), stack(3, ZS), rows(ZS)),
+        in_specs=[rows(R), rows(R), stack(2, D), stack(4, ZS), pl.BlockSpec((8, D), lambda i: (0, 0))],
+        out_specs=(rows(R), rows(R), rows(D), rows(D), stack(3, ZS), rows(ZS), *(vec(m) for m in lens)),
         compiler_params=pltpu.CompilerParams(vmem_limit_bytes=64 * 1024 * 1024 - 65536),
         name="widen",
-    )(bo, gi, gm, ga)
+    )(bo, gi, gm, ga, small)
 
 
 def body(
@@ -948,13 +958,11 @@
         gm, gatt, small = (
             lax.psum(t.astype(F32), "dp", axis_index_groups=groups) for t in (gm, gatt, small)
         )
-    block_out, grad_input, g_fc, g_proj, g_qkv, g_out = widen(block_out, grad_input, gm, gatt)
+    block_out, grad_input, g_fc, g_proj, g_qkv, g_out, *vec = widen(block_out, grad_input, gm, gatt, small)
     g_qkv = jnp.transpose(g_qkv, (2, 0, 1))
-    gbq = small[7, :ZS]
-    gbv = small[7, HC : HC + ZS]
     return (
-        block_out, grad_input, small[0], small[1], g_qkv, gbq, gbv, g_out, small[4],
-        small[2], small[3], g_fc, small[6], g_proj, small[5],
+        block_out, grad_input, vec[0], vec[1], g_qkv, vec[7], vec[8], g_out, vec[4],
+        vec[2], vec[3], g_fc, vec[6], g_proj, vec[5],
     )
 
 

time: 173 us -> 170 us (0.983)
  local copies, waits for them, and re-layouts: 2.95 us -> 0 us
    slice x2 -> x0, local copies, waits for them, and re-layouts: 2.95 us -> none  [the longest x1 1.67 us: body(): small[5]]
where the time goes in v4:
time: 170 us
  Pallas kernels  166 us (98%)
  other arithmetic  2.35 us (1%)
    pallas_call x1, Pallas kernels, body(): pl.pallas_call(kernel, out_shape=(jax.ShapeDtypeStruct((R, D), BF), jax.S...  160 us
    pallas_call x1, Pallas kernels, widen(): pl.pallas_call(widen_kernel, grid=(n,), out_shape=(jax.ShapeDtypeStruct((...  6.17 us

profile of v4, /device:TPU:1, one launch (start us, length us, event | category | flops | bytes accessed | tf_op | source)
XLA Modules:
  0.0 169.7 jit_solution(12242174092772566019)
XLA Ops:
  0.7 0.8 pad_select_fusion
  1.5 1.5 select_convert_fusion.vecs
  3.0 160.3 %layer.1 = (bf16[512,768]{1,0:T(8,128)(2,1)}, bf16[512,768]{1,0:T(8,128)(2,1)}, bf16[2,4,2,96,768]{4,3,2,1,0:T(8,128)(2,1)}, bf16[4,192,768]{2,1,0:T(8,128)(2,1)}, f32[8,768]{1,0:T(8,128)}) custom-call(s32[2]{0:T(128)} %lengths.1, f32[16,768]{1,0:T(8,128)} %select_convert_fusion.vecs, bf16[512,768]{1,0:T(8,128)(2,1)} %hid_in.1, bf16[512,768]{1,0:T(8,128)(2,1)} %og_in.1, ...), custom_call_target="tpu_custom_call" | custom-call | tf_op jit(solution)/shard_map/layer/pallas_call | solution.py:937
  163.3 6.2 %widen.1 = (bf16[512,768]{1,0:T(8,128)(2,1)}, bf16[512,768]{1,0:T(8,128)(2,1)}, f32[768,768]{1,0:T(8,128)}, f32[768,768]{1,0:T(8,128)}, f32[3,192,768]{2,1,0:T(8...) custom-call(bf16[512,768]{1,0:T(8,128)(2,1)} %get-tuple-element.35.b, ...), custom_call_target="tpu_custom_call" | custom-call | tf_op jit(solution)/shard_map/widen/pallas_call | solution.py:884
  (5 shorter events, 0.0 us)

commit v5 on v4

--- a/solution.py
+++ b/solution.py
@@ -875,7 +875,7 @@
 
 
 def widen(bo, gi, gm, ga, small):
-    n = 4
+    n = 2
     (R, D), ZS = bo.shape, ga.shape[1]
     lens = (D,) * 7 + (ZS,) * 2
     rows = lambda m: pl.BlockSpec((m // n, D), lambda i: (i, 0))

time: 170 us -> 169 us (level)
  no operation moved by 1% of the time
where the time goes in v5:
time: 169 us
  Pallas kernels  166 us (98%)
  other arithmetic  2.35 us (1%)
    pallas_call x1, Pallas kernels, body(): pl.pallas_call(kernel, out_shape=(jax.ShapeDtypeStruct((R, D), BF), jax.S...  160 us
    pallas_call x1, Pallas kernels, widen(): pl.pallas_call(widen_kernel, grid=(n,), out_shape=(jax.ShapeDtypeStruct((...  5.23 us

profile of v5, /device:TPU:1, one launch (start us, length us, event | category | flops | bytes accessed | tf_op | source)
XLA Modules:
  0.0 168.7 jit_solution(10364400608873973379)
XLA Ops:
  0.7 0.8 pad_select_fusion
  1.5 1.5 select_convert_fusion.vecs
  3.0 160.3 %layer.1 = (bf16[512,768]{1,0:T(8,128)(2,1)}, bf16[512,768]{1,0:T(8,128)(2,1)}, bf16[2,4,2,96,768]{4,3,2,1,0:T(8,128)(2,1)}, bf16[4,192,768]{2,1,0:T(8,128)(2,1)}, f32[8,768]{1,0:T(8,128)}) custom-call(s32[2]{0:T(128)} %lengths.1, f32[16,768]{1,0:T(8,128)} %select_convert_fusion.vecs, bf16[512,768]{1,0:T(8,128)(2,1)} %hid_in.1, bf16[512,768]{1,0:T(8,128)(2,1)} %og_in.1, ...), custom_call_target="tpu_custom_call" | custom-call | tf_op jit(solution)/shard_map/layer/pallas_call | solution.py:937
  163.3 5.2 %widen.1 = (bf16[512,768]{1,0:T(8,128)(2,1)}, bf16[512,768]{1,0:T(8,128)(2,1)}, f32[768,768]{1,0:T(8,128)}, f32[768,768]{1,0:T(8,128)}, f32[3,192,768]{2,1,0:T(8...) custom-call(bf16[512,768]{1,0:T(8,128)(2,1)} %get-tuple-element.35.b, ...), custom_call_target="tpu_custom_call" | custom-call | tf_op jit(solution)/shard_map/widen/pallas_call | solution.py:884
  (5 shorter events, 0.0 us)
